TPU v7x, 128 devices: a whole 4x4x4 slice. The times are simulated.
128 devices in a mesh: section: 8 (over z, x_hi), tensor: 16 (over y, x_lo, core).
Axes of the slice: x: 4 (x_hi: 2, x_lo: 2; x = x_hi * 2 + x_lo), y: 4, z: 4, core: 2. Of those that a mesh axis runs over, the one named last changes fastest.
Arguments:
- forward_in: bfloat16 [8, 768, 6144], P('section', 'tensor'), may hold values from -6 to 6
- grad_out: bfloat16 [8, 768, 6144], P('section', 'tensor'), may hold values from -1.1953125 to 1.1953125
- saved_in: bfloat16 [8, 768, 6144], P('section', 'tensor'), may hold values from -6 to 6
- weight: bfloat16 [8, 6144, 6144], P('section', 'tensor'), may hold values from -0.078125 to 0.078125
- gain: bfloat16 [8, 6144], P('section', 'tensor'), may hold values from 0.099609375 to 1.8984375
Outputs:
- next_input: bfloat16 [8, 768, 6144], P('section', 'tensor')
- prev_grad: bfloat16 [8, 768, 6144], P('section', 'tensor')
- weight_grad: bfloat16 [8, 6144, 6144], P('section', 'tensor')
- gain_grad: float32 [8, 6144], P('section', 'tensor')
All inputs are finite; a program needn't handle non-finite values.
Results may differ from a plain program's by a relative error of at most 0.019.
Values may be sent and summed in bfloat16 or wider, within the bound.
A program may use at most 192 MiB of HBM per device.

v0:
```python
import jax
import jax.numpy as jnp
from jax import lax
from jax.sharding import PartitionSpec as P


def passed_along(value, axis, steps):
    count = lax.axis_size(axis)
    pairs = [(source, (source + steps) % count) for source in range(count)]
    return lax.ppermute(value, axis, pairs)


def partner(shard, axis, apart):
    return lax.ppermute(shard, axis, [(i, i ^ 1 << apart) for i in range(lax.axis_size(axis))])


def normalize(values):
    center = jnp.mean(values, axis=1, keepdims=True)
    shifted = values - center
    recip = lax.rsqrt(jnp.mean(shifted * shifted, axis=1, keepdims=True) + 1e-05)
    return (shifted * recip, recip)


def neighbour(values, offset):
    return passed_along(values, "section", offset)


def local(forward_in, grad_out, saved_in, weight, gain):
    layer_in = forward_in[0]
    upstream = grad_out[0]
    stored = saved_in[0]
    matrix = weight[0]
    scales = gain[0]
    width_local = matrix.shape[0]
    tensor_index = lax.axis_index("tensor")
    col_start = tensor_index * width_local
    scale_local = scales.astype(jnp.float32)
    bit_total = lax.axis_size("section").bit_length() - 1
    bit_order = list(range(bit_total))
    fetched = stored
    for bit_number in bit_order:
        fetched = partner(fetched, "section", bit_number)
    layer_all, upstream_all, saved_all, scales_all = (
        lax.all_gather(layer_in, "tensor", axis=0, tiled=True),
        lax.all_gather(upstream, "tensor", axis=0, tiled=True),
        lax.all_gather(fetched, "tensor", axis=0, tiled=True),
        lax.all_gather(scales, "tensor", axis=0, tiled=True),
    )
    normed, ignored = normalize(layer_all.astype(jnp.float32))
    hidden = (lax.dynamic_slice_in_dim(normed, col_start, width_local, 1) * scale_local).astype(
        jnp.bfloat16
    )
    own_sums = lax.psum_scatter(
        jnp.dot(hidden, matrix, preferred_element_type=jnp.float32).astype(jnp.bfloat16),
        "tensor",
        scatter_dimension=0,
        tiled=True,
    ).astype(jnp.float32)
    produced = (layer_in.astype(jnp.float32) + own_sums).astype(jnp.bfloat16)
    saved_normed, ignored = normalize(saved_all.astype(jnp.float32))
    normed_local = lax.dynamic_slice_in_dim(saved_normed, col_start, width_local, 1)
    hidden_local = (normed_local * scale_local).astype(jnp.bfloat16)
    grad_hidden = jnp.einsum("td,cd->tc", upstream_all, matrix, preferred_element_type=jnp.float32)
    gain_grad = jnp.sum(grad_hidden * normed_local, axis=0)
    weight_grad = jnp.einsum(
        "tc,td->cd", hidden_local, upstream_all, preferred_element_type=jnp.float32
    ).astype(jnp.bfloat16)
    grad_rows = lax.all_to_all(
        grad_hidden.astype(jnp.bfloat16), "tensor", split_axis=0, concat_axis=1, tiled=True
    )
    own_normed, own_recip = normalize(fetched.astype(jnp.float32))
    grad_normed = grad_rows.astype(jnp.float32) * scales_all.astype(jnp.float32)
    inner = (
        grad_normed
        - jnp.mean(grad_normed, axis=1, keepdims=True)
        - own_normed * jnp.mean(grad_normed * own_normed, axis=1, keepdims=True)
    )
    grad_in = (upstream.astype(jnp.float32) + own_recip * inner).astype(jnp.bfloat16)
    next_input = neighbour(produced, 1)
    prev_grad = neighbour(grad_in, -1)
    return (next_input[None], prev_grad[None], weight_grad[None], gain_grad[None])


def solution(mesh):
    return jax.shard_map(
        local,
        mesh=mesh,
        in_specs=(
            P("section", "tensor", None),
            P("section", "tensor", None),
            P("section", "tensor", None),
            P("section", "tensor", None),
            P("section", "tensor"),
        ),
        out_specs=(
            P("section", "tensor", None),
            P("section", "tensor", None),
            P("section", "tensor", None),
            P("section", "tensor"),
        ),
        check_vma=False,
    )
```

profile of v0, /device:TPU:1, one launch (start us, length us, event | category | flops | bytes accessed | tf_op | source)
XLA Modules:
  0.0 346.6 jit_solution(6912018383230809373)
XLA Ops:
  8.0 3.7 %collective-permute-start.1 = (bf16[48,6144]{1,0:T(8,128)(2,1)}, bf16[48,6144]{1,0:T(8,128)(2,1)S(1)}, u32[]{:S(2)}, u32[]{:S(2)}) collective-permute-start(bf16[48,6144]{1,0:T(8,128)(2,1)} %bitcast.47), channel_id=1, source_target_pairs={{0,16},{16,0},{32,48},{48,32},{64,80},{80,64},{96,112},{112,96},{1... | collective-permute-start | bytes 1769480 | tf_op jit(solution)/shard_map/ppermute | solution.py:14
  11.6 13.9 %collective-permute-done.1 = bf16[48,6144]{1,0:T(8,128)(2,1)S(1)} collective-permute-done((bf16[48,6144]{1,0:T(8,128)(2,1)}, bf16[48,6144]{1,0:T(8,128)(2,1)S(1)}, u32[]{:S(2)}, u32[]{:S(2)}) %collective-permute-start.1) | collective-permute-done | bytes 589856 | tf_op jit(solution)/shard_map/ppermute | solution.py:14
  25.5 1.8 collective-permute-start.2
  27.3 9.9 %collective-permute-done.2 = bf16[48,6144]{1,0:T(8,128)(2,1)S(1)} collective-permute-done((bf16[48,6144]{1,0:T(8,128)(2,1)S(1)}, bf16[48,6144]{1,0:T(8,128)(2,1)S(1)}, u32[]{:S(2)}, u32[]{:S(2)}) %collective-permute-start.2) | collective-permute-done | bytes 589856 | tf_op jit(solution)/shard_map/ppermute | solution.py:14
  37.2 4.0 %collective-permute-start.3 = (bf16[48,6144]{1,0:T(8,128)(2,1)S(1)}, bf16[48,6144]{1,0:T(8,128)(2,1)S(1)}, u32[]{:S(2)}, u32[]{:S(2)}) collective-permute-start(bf16[48,6144]{1,0:T(8,128)(2,1)S(1)} %collective-permute-done.2), channel_id=1, source_target_pairs={{0,64},{16,80},{32,96},{48,112},{64,0},{80,16},{96,32},{112,48},{1... | collective-permute-start | bytes 1769480 | tf_op jit(solution)/shard_map/ppermute | solution.py:14
  41.2 12.8 %collective-permute-done.3 = bf16[48,6144]{1,0:T(8,128)(2,1)S(1)} collective-permute-done((bf16[48,6144]{1,0:T(8,128)(2,1)S(1)}, bf16[48,6144]{1,0:T(8,128)(2,1)S(1)}, u32[]{:S(2)}, u32[]{:S(2)}) %collective-permute-start.3) | collective-permute-done | bytes 589856 | tf_op jit(solution)/shard_map/ppermute | solution.py:14
  55.6 16.4 %all-gather.9.cloned.1.call-done = bf16[1,768,6144]{2,1,0:T(8,128)(2,1)} async-done(((bf16[1,48,6144]{2,1,0:T(8,128)(2,1)}), bf16[1,768,6144]{2,1,0:T(8,128)(2,1)}) %all-gather.9.cloned.1.call-update) | async-done | bytes 9437200 | tf_op jit(solution)/shard_map/all_gather | solution.py:44
  72.0 5.0 %convert_reduce_fusion = f32[768]{0:T(1024)S(1)} fusion(bf16[1,768,6144]{2,1,0:T(8,128)(2,1)} %all-gather.9.cloned.1.call-done), kind=kLoop, calls=%fused_computation | loop fusion | flops 9436416 | bytes 9440256 | tf_op jit(solution)/shard_map/reduce_sum | solution.py:18
  77.0 12.9 %multiply_reduce_fusion.1 = (f32[768]{0:T(1024)S(1)}, f32[768,6144]{1,0:T(8,128)}) fusion(f32[768]{0:T(1024)S(1)} %broadcast_multiply_fusion.1, bf16[1,768,6144]{2,1,0:T(8,128)(2,1)} %all-gather.9.cloned.1.call-done), kind=kLoop, calls=%fused_computation.6 | loop fusion | flops 18873600 | bytes 28317696 | tf_op jit(solution)/shard_map/reduce_sum | solution.py:20
  90.0 10.3 %convolution_convert_fusion = bf16[768,6144]{1,0:T(8,128)(2,1)} fusion(bf16[1,384,6144]{2,1,0:T(8,128)(2,1)} %param.8, f32[768,6144]{1,0:T(8,128)} %get-tuple-element.7, s32[]{:T(128)S(6)} %select_n.4, f32[768]{0:T(1024)S(1)} %add_rsqrt_fusion.1, f32[384]{0:T(512)S(1)} %convert_reduce_fusion.3), kind=kOutput, calls=%fused_computation.7 | convolution fusion | flops 3629481984 | bytes 15340036 | tf_op jit(solution)/shard_map/dot_general | solution.py:54
  100.3 20.4 %all-gather.2 = bf16[1,6144]{1,0:T(2,128)(2,1)S(1)} all-gather(bf16[1,384]{1,0:T(2,128)(2,1)S(1)} %copy-done.4), channel_id=4, replica_groups=mesh['section'=8,'tensor'=16] {'tensor'}, dimensions={1}, use_global_device_ids=true | all-gather | bytes 13056 | tf_op jit(solution)/shard_map/all_gather | solution.py:47
  121.0 11.8 %all-gather.7.cloned.1.call-done = bf16[768,6144]{1,0:T(8,128)(2,1)} async-done(((bf16[48,6144]{1,0:T(8,128)(2,1)}), bf16[768,6144]{1,0:T(8,128)(2,1)}) %all-gather.7.cloned.1.call-update) | async-done | bytes 9437200 | tf_op jit(solution)/shard_map/all_gather | solution.py:46
  132.8 5.0 %convert_reduce_fusion.1 = f32[768]{0:T(1024)S(1)} fusion(bf16[768,6144]{1,0:T(8,128)(2,1)} %all-gather.7.cloned.1.call-done), kind=kLoop, calls=%fused_computation.3 | loop fusion | flops 9436416 | bytes 9440256 | tf_op jit(solution)/shard_map/reduce_sum | solution.py:18
  137.8 12.7 %multiply_reduce_fusion = (f32[768]{0:T(1024)S(1)}, f32[768,6144]{1,0:T(8,128)}) fusion(f32[768]{0:T(1024)S(1)} %broadcast_multiply_fusion, bf16[768,6144]{1,0:T(8,128)(2,1)} %all-gather.7.cloned.1.call-done), kind=kLoop, calls=%fused_computation.5 | loop fusion | flops 18873600 | bytes 28317696 | tf_op jit(solution)/shard_map/reduce_sum | solution.py:20
  150.5 41.9 %all-gather.11.cloned.1.call-done = bf16[1,768,6144]{2,1,0:T(8,128)(2,1)} async-done(((bf16[1,48,6144]{2,1,0:T(8,128)(2,1)}), bf16[1,768,6144]{2,1,0:T(8,128)(2,1)}) %all-gather.11.cloned.1.call-update) | async-done | bytes 9437200 | tf_op jit(solution)/shard_map/all_gather | solution.py:45
  192.4 9.9 %multiply_reduce_fusion.2 = (f32[384]{0:T(512)S(1)}, bf16[768,384]{1,0:T(8,128)(2,1)}) fusion(f32[768,6144]{1,0:T(8,128)} %get-tuple-element.5, s32[]{:T(128)S(6)} %select_n.4, f32[768]{0:T(1024)S(1)} %add_rsqrt_fusion, bf16[1,384,6144]{2,1,0:T(8,128)(2,1)} %param.8, bf16[1,768,6144]{2,1,0:T(8,128)(2,1)} %all-gather.11.cloned.1.call-done), kind=kOutput, calls=%fused_computation.37 | convolution fusion | flops 3625057792 | bytes 15929860 | tf_op jit(solution)/shard_map/td,cd->tc/dot_general | solution.py:63
  202.3 5.1 %all-to-all-start = ((bf16[16,48,384]{2,1,0:T(8,128)(2,1)}), bf16[16,48,384]{2,1,0:T(8,128)(2,1)S(1)}, u32[]{:S(2)}, u32[]{:S(2)}) async-start(bf16[16,48,384]{2,1,0:T(8,128)(2,1)} %bitcast.7), calls=%async_computation.1 | async-start | bytes 1179648 | tf_op jit(solution)/shard_map/all_to_all | solution.py:68
  208.4 16.6 %all-to-all-done = bf16[16,48,384]{2,1,0:T(8,128)(2,1)S(1)} async-done(((bf16[16,48,384]{2,1,0:T(8,128)(2,1)}), bf16[16,48,384]{2,1,0:T(8,128)(2,1)S(1)}, u32[]{:S(2)}, u32[]{:S(2)}) %all-to-all-start) | async-done | bytes 589856 | tf_op jit(solution)/shard_map/all_to_all | solution.py:68
  226.6 4.9 %collective-permute-start.4 = (bf16[48,6144]{1,0:T(8,128)(2,1)S(1)}, bf16[48,6144]{1,0:T(8,128)(2,1)S(1)}, u32[]{:S(2)}, u32[]{:S(2)}) collective-permute-start(bf16[48,6144]{1,0:T(8,128)(2,1)S(1)} %fusion.21), channel_id=1, source_target_pairs={{0,112},{16,0},{32,16},{48,32},{64,48},{80,64},{96,80},{112,96},{1... | collective-permute-start | bytes 1769480 | tf_op jit(solution)/shard_map/ppermute | solution.py:10
  231.5 89.4 %reduce-scatter.2.cloned.1.call-done = bf16[48,6144]{1,0:T(8,128)(2,1)} async-done(((bf16[768,6144]{1,0:T(8,128)(2,1)}), bf16[48,6144]{1,0:T(8,128)(2,1)}) %reduce-scatter.2.cloned.1.call-update) | async-done | bytes 589840 | tf_op jit(solution)/shard_map/reduce_scatter | solution.py:53
  320.9 1.2 fusion.26
  322.1 2.7 collective-permute-start
  324.8 10.2 %fusion.8 = bf16[1,384,6144]{2,1,0:T(8,128)(2,1)} fusion(bf16[1,768,6144]{2,1,0:T(8,128)(2,1)} %all-gather.11.cloned.1.call-done, f32[768,6144]{1,0:T(8,128)} %get-tuple-element.5, s32[]{:T(128)S(6)} %select_n.4, f32[768]{0:T(1024)S(1)} %add_rsqrt_fusion, f32[384]{0:T(512)S(1)} %convert_reduce_fusion.3), kind=kOutput, calls=%fused_computation.13 | convolution fusion | flops 3627122688 | bytes 15340036 | tf_op jit(solution)/shard_map/tc,td->cd/dot_general | solution.py:65
  335.1 3.4 collective-permute-done
  (40 shorter events, 7.0 us)
Async XLA Ops:
  7.2 48.4 %copy-start.4 = (bf16[1,384]{1,0:T(2,128)(2,1)S(1)}, bf16[1,384]{1,0:T(2,128)(2,1)}, u32[]{:S(2)}) copy-start(bf16[1,384]{1,0:T(2,128)(2,1)} %param.9) | copy-start | bytes 2308
  7.2 64.8 %all-gather.9.cloned.1.call-start = ((), (), s32[]{:S(2)}) async-start(), calls=%async_computation.4 | async-start | bytes 10027008 | tf_op jit(solution)/shard_map/all_gather | solution.py:44
  7.9 124.9 %all-gather.7.cloned.1.call-start = ((), (), s32[]{:S(2)}) async-start(), calls=%async_computation.3 | async-start | bytes 10027008 | tf_op jit(solution)/shard_map/all_gather | solution.py:46
  8.0 17.5 %collective-permute-start.1 = (bf16[48,6144]{1,0:T(8,128)(2,1)}, bf16[48,6144]{1,0:T(8,128)(2,1)S(1)}, u32[]{:S(2)}, u32[]{:S(2)}) collective-permute-start(bf16[48,6144]{1,0:T(8,128)(2,1)} %bitcast.47), channel_id=1, source_target_pairs={{0,16},{16,0},{32,48},{48,32},{64,80},{80,64},{96,112},{112,96},{1... | collective-permute-start | bytes 1769480 | tf_op jit(solution)/shard_map/ppermute | solution.py:14
  25.5 11.7 %collective-permute-start.2 = (bf16[48,6144]{1,0:T(8,128)(2,1)S(1)}, bf16[48,6144]{1,0:T(8,128)(2,1)S(1)}, u32[]{:S(2)}, u32[]{:S(2)}) collective-permute-start(bf16[48,6144]{1,0:T(8,128)(2,1)S(1)} %collective-permute-done.1), channel_id=1, source_target_pairs={{0,32},{16,48},{32,0},{48,16},{64,96},{80,112},{96,64},{112,80},{1... | collective-permute-start | bytes 1769480 | tf_op jit(solution)/shard_map/ppermute | solution.py:14
  37.2 16.8 %collective-permute-start.3 = (bf16[48,6144]{1,0:T(8,128)(2,1)S(1)}, bf16[48,6144]{1,0:T(8,128)(2,1)S(1)}, u32[]{:S(2)}, u32[]{:S(2)}) collective-permute-start(bf16[48,6144]{1,0:T(8,128)(2,1)S(1)} %collective-permute-done.2), channel_id=1, source_target_pairs={{0,64},{16,80},{32,96},{48,112},{64,0},{80,16},{96,32},{112,48},{1... | collective-permute-start | bytes 1769480 | tf_op jit(solution)/shard_map/ppermute | solution.py:14
  54.0 0.8 copy-start
  54.8 137.6 %all-gather.11.cloned.1.call-start = ((), (), s32[]{:S(2)}) async-start(), calls=%async_computation.5 | async-start | bytes 10027008 | tf_op jit(solution)/shard_map/all_gather | solution.py:45
  55.5 265.4 %reduce-scatter.2.cloned.1.call-start = ((), (), s32[]{:S(2)}) async-start(), calls=%async_computation.2 | async-start | bytes 10027008 | tf_op jit(solution)/shard_map/reduce_scatter | solution.py:53
  100.3 20.5 %copy-start.1 = (bf16[48,6144]{1,0:T(8,128)(2,1)S(1)}, bf16[48,6144]{1,0:T(8,128)(2,1)}, u32[]{:S(2)}) copy-start(bf16[48,6144]{1,0:T(8,128)(2,1)} %copy-done) | copy-start | bytes 1769476
  202.3 22.6 %all-to-all-start = ((bf16[16,48,384]{2,1,0:T(8,128)(2,1)}), bf16[16,48,384]{2,1,0:T(8,128)(2,1)S(1)}, u32[]{:S(2)}, u32[]{:S(2)}) async-start(bf16[16,48,384]{2,1,0:T(8,128)(2,1)} %bitcast.7), calls=%async_computation.1 | async-start | bytes 1179648 | tf_op jit(solution)/shard_map/all_to_all | solution.py:68
  225.1 1.1 copy-start.2
  226.1 94.7 %copy-start.3 = (bf16[1,48,6144]{2,1,0:T(8,128)(2,1)S(1)}, bf16[1,48,6144]{2,1,0:T(8,128)(2,1)}, u32[]{:S(2)}) copy-start(bf16[1,48,6144]{2,1,0:T(8,128)(2,1)} %param.5) | copy-start | bytes 1769476
  226.6 108.4 %collective-permute-start.4 = (bf16[48,6144]{1,0:T(8,128)(2,1)S(1)}, bf16[48,6144]{1,0:T(8,128)(2,1)S(1)}, u32[]{:S(2)}, u32[]{:S(2)}) collective-permute-start(bf16[48,6144]{1,0:T(8,128)(2,1)S(1)} %fusion.21), channel_id=1, source_target_pairs={{0,112},{16,0},{32,16},{48,32},{64,48},{80,64},{96,80},{112,96},{1... | collective-permute-start | bytes 1769480 | tf_op jit(solution)/shard_map/ppermute | solution.py:10
  322.1 16.4 %collective-permute-start = (bf16[48,6144]{1,0:T(8,128)(2,1)S(1)}, bf16[48,6144]{1,0:T(8,128)(2,1)S(1)}, u32[]{:S(2)}, u32[]{:S(2)}) collective-permute-start(bf16[48,6144]{1,0:T(8,128)(2,1)S(1)} %fusion.26), channel_id=1, source_target_pairs={{0,16},{16,32},{32,48},{48,64},{64,80},{80,96},{96,112},{112,0},{1... | collective-permute-start | bytes 1769480 | tf_op jit(solution)/shard_map/ppermute | solution.py:10
Sparse Core Ops, SparseCore 0:
  9.7 62.2 all-gather.8
  74.3 58.4 all-gather.6
  134.5 57.8 all-gather.10
  194.7 126.1 reduce-scatter.1
where the time goes:
time: 349 us; the launch traced here: 347 us
  waiting for transfers between devices  217 us (62%)
  other arithmetic  38.8 us (11%)
  matrix products  30.5 us (9%)
  starting transfers between devices  22.2 us (6%)
  blocking collectives  20.4 us (6%)
  between operations  13.9 us (4%)
    reduce_scatter x1, waiting for transfers between devices, local(): lax.psum_scatter(jnp.dot(hidden, matrix, preferred_element_type=jnp.float...  89.4 us
    all_gather x1, waiting for transfers between devices, local(): lax.all_gather(upstream, 'tensor', axis=0, tiled=True)  41.9 us
    ppermute x3, waiting for transfers between devices, partner(): lax.ppermute(shard, axis, [(i, i ^ 1 << apart) for i in range(lax.axis_si...  36.6 us
    reduce_sum x3, other arithmetic, normalize(): jnp.mean(shifted * shifted, axis=1, keepdims=True) + 1e-05  26 us
    all_gather x1, blocking collectives, local(): lax.all_gather(scales, 'tensor', axis=0, tiled=True)  20.4 us
    all_to_all x1, waiting for transfers between devices, local(): lax.all_to_all(grad_hidden.astype(jnp.bfloat16), 'tensor', split_axis=0,...  16.6 us
    all_gather x1, waiting for transfers between devices, local(): lax.all_gather(layer_in, 'tensor', axis=0, tiled=True)  16.4 us
    all_gather x1, waiting for transfers between devices, local(): lax.all_gather(fetched, 'tensor', axis=0, tiled=True)  11.8 us
  transfers between devices with their start and end apart: 10, of which 9 were waited for; matrix products, arithmetic and copies ran while one was open for 20% of the time, Pallas kernels for 0%

commit v1 on v0

v1 whole, which is shorter than its diff:
```python
import jax
import jax.numpy as jnp
from jax import lax
from jax.experimental import pallas as pl
from jax.experimental.pallas import tpu as pltpu
from jax.sharding import PartitionSpec as P

D = 6144
TOKENS = 768
ROWS = 48
CHIP = 96
WIDTH = 384
HALF = D // 2
CA = 1280
CB = HALF - CA
STRIP = 16
BF = jnp.bfloat16
F32 = jnp.float32
EPS = 1e-05


def block(r, d):
    return (r * 4 + d) * CHIP


def normalize(values):
    center = jnp.mean(values, axis=1, keepdims=True)
    shifted = values - center
    recip = lax.rsqrt(jnp.mean(shifted * shifted, axis=1, keepdims=True) + EPS)
    return shifted * recip, recip


def strips(rows, body):
    def step(i, carry):
        body(pl.ds(pl.multiple_of(i * STRIP, STRIP), STRIP), i)
        return carry

    lax.fori_loop(0, rows // STRIP, step, 0)


def kernel(
    x_ref, g_ref, s_ref, w_ref, gain_ref,
    next_ref, prev_ref, wg_ref, gg_ref,
    G, W, WC, PF, HN, XR, XO, NX, SO, NS, SR, BHT, DH, GI, XRES,
    SA, RA, SA2, RA2, SAF, RAF, SB2, RB2, SBF, RBF, SBX, RBX, OA, OB,
    QC, QS, QR, EC, ES, ER,
    send_sem, recv_sem, local_sem, group_sem,
):
    s = lax.axis_index("section")
    t = lax.axis_index("tensor")
    y, xl, c = t // 4, (t // 2) % 2, t % 2
    sib = (s, t + 1 - 2 * c)
    yp = (s, ((y + 1) % 4) * 4 + xl * 2 + c)
    ym = (s, ((y + 3) % 4) * 4 + xl * 2 + c)
    pair = (s, y * 4 + (1 - xl) * 2 + c)
    mirrored, following, previous = 7 - s, (s + 1) % 8, (s + 7) % 8

    def columns(start, width):
        return pl.ds(pl.multiple_of(start, 128), width)

    mine = c * HALF
    other = (1 - c) * HALF
    cols_a = columns(mine, CA)
    cols_b = columns(mine + CA, CB)

    names = {}
    sent = []

    def send(name, src, dst, device, landing=None):
        i = names.setdefault(name, (len(names), dst if landing is None else landing))[0]
        copy = pltpu.make_async_remote_copy(
            src_ref=src, dst_ref=dst, send_sem=send_sem.at[i], recv_sem=recv_sem.at[i],
            device_id=device, device_id_type=pl.DeviceIdType.MESH,
        )
        copy.start()
        sent.append(copy)

    def arrived(ref, sem, scratch_sem):
        pltpu.make_async_remote_copy(
            src_ref=ref, dst_ref=ref, send_sem=scratch_sem, recv_sem=sem,
            device_id=sib, device_id_type=pl.DeviceIdType.MESH,
        ).wait_recv()

    def left(ref, sem, scratch_sem):
        pltpu.make_async_remote_copy(
            src_ref=ref, dst_ref=ref, send_sem=sem, recv_sem=scratch_sem,
            device_id=sib, device_id_type=pl.DeviceIdType.MESH,
        ).wait_send()

    def recv(name):
        i, landing = names[name]
        arrived(landing, recv_sem.at[i], send_sem.at[i])

    X_IN, X_OUT, S_IN, S_OUT, Q_IN, Q_OUT, E_IN, E_OUT, G_IN, G_OUT, P_IN, P_OUT, N_IN, N_OUT = range(14)

    def grouped(src, dst, out, into, device):
        pltpu.make_async_remote_copy(
            src_ref=src, dst_ref=dst, send_sem=group_sem.at[out], recv_sem=group_sem.at[into],
            device_id=device, device_id_type=pl.DeviceIdType.MESH,
        ).start()

    load_x = pltpu.make_async_copy(x_ref, XO, local_sem.at[0])
    load_g = pltpu.make_async_copy(g_ref, G.at[pl.ds(pl.multiple_of(c * ROWS, 16), ROWS), :], local_sem.at[1])
    load_s = pltpu.make_async_copy(s_ref, SO, local_sem.at[2])
    load_w = pltpu.make_async_copy(w_ref, W, local_sem.at[3])
    load_wc = pltpu.make_async_copy(w_ref.at[:, columns(mine, HALF)], WC.at[0:WIDTH, :], local_sem.at[4])
    load_xres = pltpu.make_async_copy(
        x_ref.at[:, columns(mine, HALF)], XRES.at[pl.ds(pl.multiple_of(c * ROWS, 16), ROWS), :], local_sem.at[5]
    )
    for load in (load_x, load_g, load_s, load_wc, load_xres, load_w):
        load.start()

    barrier = pltpu.get_barrier_semaphore()

    def greet(section, first):
        def step(i, carry):
            pl.semaphore_signal(
                barrier, inc=1, device_id=(section, (t + i) % 16), device_id_type=pl.DeviceIdType.MESH
            )
            return carry

        lax.fori_loop(first, 16, step, 0)

    greet(s, 1)
    greet(mirrored, 0)
    greet(following, 0)
    greet(previous, 0)

    load_x.wait()

    def norm_x(rows, i):
        NX[rows, :] = normalize(XO[rows, :].astype(F32))[0].astype(BF)

    strips(ROWS, norm_x)

    pl.semaphore_wait(barrier, 63)

    own_rows = pl.ds(pl.multiple_of(c * ROWS, 16), ROWS)
    send("g_half", g_ref.at[:, columns(other, HALF)], G.at[own_rows, columns(other, HALF)], sib)
    send("w_half", w_ref.at[:, columns(other, HALF)], WC.at[WIDTH : 2 * WIDTH, :], sib)
    send("x_half", x_ref.at[:, columns(other, HALF)], XRES.at[own_rows, :], sib)
    send("g_rest", g_ref.at[:, columns(mine, HALF)], G.at[own_rows, columns(mine, HALF)], sib)

    def slot_at(target):
        d = (y + 4 - target // 4) % 4
        r = (xl + (target // 2) % 2) % 2
        return (r * 4 + d) * 2 + c

    def slot_rows(slot):
        return pl.ds(pl.multiple_of(slot * ROWS, 16), ROWS)

    own_x = pltpu.make_async_copy(
        NX.at[:, columns(t * WIDTH, WIDTH)], XR.at[slot_rows(c), :], group_sem.at[X_IN]
    )
    own_x.start()

    def send_x(i, carry):
        target = (t + i) % 16
        grouped(
            NX.at[:, columns(target * WIDTH, WIDTH)], XR.at[slot_rows(slot_at(target)), :], X_OUT, X_IN, (s, target)
        )
        return carry

    lax.fori_loop(1, 16, send_x, 0)

    load_g.wait()
    recv("g_half")

    def own(cols, r=0, d=0, first=0, rows=CHIP):
        return G.at[block(r, d) + first : block(r, d) + first + rows, cols]

    send("a_p", own(cols_a), own(cols_a, 0, 3), yp)
    send("a_m", own(cols_a), own(cols_a, 0, 1), ym)
    send("b_x", own(cols_b), own(cols_b, 1, 0), pair)
    send("a_x0", own(cols_a), own(cols_a, 1, 0), pair)
    send("b_p", own(cols_b), own(cols_b, 0, 3), yp)
    send("b_m", own(cols_b), own(cols_b, 0, 1), ym)

    load_s.wait()
    QC[...] = jnp.zeros(QC.shape, F32)

    def norm_s(rows, i):
        normed, recip = normalize(SO[rows, :].astype(F32))
        NS[rows, :] = normed.astype(BF)
        QC[rows, :] = jnp.broadcast_to(recip, (STRIP, 128))

    strips(ROWS, norm_s)
    QS[...] = QC[...].T[0:8, :]

    def send_s(i, carry):
        target = (t + i) % 16
        slot = slot_at(target)
        grouped(
            NS.at[:, columns(target * WIDTH, WIDTH)], SR.at[slot_rows(slot), :], S_OUT, S_IN, (mirrored, target)
        )
        grouped(QS, QR.at[slot], Q_OUT, Q_IN, (mirrored, target))
        return carry

    lax.fori_loop(0, 16, send_s, 0)

    def to_sibling(cols, r, d, first=0, rows=CHIP):
        ref = own(cols, r, d, first, rows)
        grouped(ref, ref, G_OUT, G_IN, sib)

    recv("a_p")
    send("a_pp", own(cols_a, 0, 3, 0, ROWS), own(cols_a, 0, 2, 0, ROWS), yp)
    send("a_x3", own(cols_a, 0, 3), own(cols_a, 1, 3), pair)
    to_sibling(cols_a, 0, 3)
    recv("a_m")
    send("a_mm", own(cols_a, 0, 1, ROWS, ROWS), own(cols_a, 0, 2, ROWS, ROWS), ym)
    send("a_x1", own(cols_a, 0, 1), own(cols_a, 1, 1), pair)
    to_sibling(cols_a, 0, 1)
    recv("b_x")
    send("bx_p", own(cols_b, 1, 0), own(cols_b, 1, 3), yp)
    send("bx_m", own(cols_b, 1, 0), own(cols_b, 1, 1), ym)
    to_sibling(cols_b, 1, 0)

    arrived(XR, group_sem.at[X_IN], group_sem.at[X_OUT])
    scale = gain_ref[...].astype(F32)

    def make_hidden(rows, i):
        HN[rows, 0:WIDTH] = (XR[rows, :].astype(F32) * scale).astype(BF)

    strips(TOKENS, make_hidden)
    send("hidden", HN.at[:, 0:WIDTH], HN.at[:, WIDTH : 2 * WIDTH], sib)
    load_wc.wait()
    load_xres.wait()
    recv("w_half")
    recv("x_half")
    recv("hidden")

    def project(first, rows, start, width, step, store):
        def tile(i, carry):
            at = pl.multiple_of(start + i * step, 128)
            store(
                pl.multiple_of(i * step, 128),
                jnp.dot(HN[first : first + rows, :], WC[:, pl.ds(at, step)], preferred_element_type=F32),
            )
            return carry

        lax.fori_loop(0, width // step, tile, 0)

    def store_pair(at, value):
        here = pl.ds(at, 256)
        SA[0:CHIP, here] = (value[0:CHIP] + XRES[:, here].astype(F32)).astype(BF)
        SA[CHIP : 4 * CHIP, here] = value[CHIP : 4 * CHIP].astype(BF)

    project(0, 4 * CHIP, 0, CA, 256, store_pair)
    for d in (2, 1, 3, 0):
        send("ra%d" % d, SA.at[d * CHIP : (d + 1) * CHIP, :], RA.at[d * CHIP : (d + 1) * CHIP, :], pair)

    recv("b_p")
    send("b_pp", own(cols_b, 0, 3), own(cols_b, 0, 2), yp)
    to_sibling(cols_b, 0, 3)
    recv("bx_m")
    send("bx_mm", own(cols_b, 1, 1), own(cols_b, 1, 2), ym)
    to_sibling(cols_b, 1, 1)
    recv("a_pp")
    recv("a_mm")
    send("a_x2", own(cols_a, 0, 2), own(cols_a, 1, 2), pair)
    to_sibling(cols_a, 0, 2)
    recv("b_m")
    to_sibling(cols_b, 0, 1)
    recv("bx_p")
    to_sibling(cols_b, 1, 3)

    def store_b(at, value):
        PF[:, pl.ds(pl.multiple_of(CA + at, 128), 256)] = value

    project(0, TOKENS, CA, CB, 256, store_b)

    def combine(dst, terms, first=0, rows=CHIP):
        def body(at, i):
            total = None
            for ref, base, cols in terms:
                here = pl.ds(pl.multiple_of(base + first + i * STRIP, STRIP), STRIP)
                value = ref[here, cols].astype(F32)
                total = value if total is None else total + value
            ref, base = dst
            ref[pl.ds(pl.multiple_of(base + first + i * STRIP, STRIP), STRIP), :] = total.astype(BF)

        strips(rows, body)

    in_a, in_b = slice(0, CA), slice(CA, HALF)
    all_a, all_b = slice(0, CA), slice(0, CB)

    def part(ref, base, first=0, rows=CHIP):
        return ref.at[base + first : base + first + rows, :]

    combine((SB2, 0), [(PF, block(0, 2), in_b)])
    send("rb2p", part(SB2, 0), part(RB2, 0), yp)
    combine((SB2, CHIP), [(PF, block(1, 2), in_b)])
    send("rb2m", part(SB2, CHIP), part(RB2, CHIP), ym)
    combine((SBF, CHIP), [(PF, block(1, 1), in_b)])
    send("rbf01", part(SBF, CHIP), part(RBF, CHIP), yp)
    combine((SBF, 2 * CHIP), [(PF, block(0, 3), in_b)])
    send("rbf10", part(SBF, 2 * CHIP), part(RBF, 2 * CHIP), ym)

    def store_a(at, value):
        PF[4 * CHIP : 8 * CHIP, pl.ds(at, 256)] = value

    project(4 * CHIP, 4 * CHIP, 0, CA, 256, store_a)

    recv("ra2")
    combine((SA2, 0), [(PF, block(1, 2), in_a), (RA, 2 * CHIP, all_a)])
    send("ra2p", part(SA2, 0, 0, ROWS), part(RA2, 0, 0, ROWS), yp)
    send("ra2m", part(SA2, 0, ROWS, ROWS), part(RA2, 0, ROWS, ROWS), ym)
    recv("ra1")
    combine((SAF, 0), [(PF, block(1, 1), in_a), (RA, CHIP, all_a)], ROWS, ROWS)
    send("rafp1", part(SAF, 0, ROWS, ROWS), part(RAF, 0, ROWS, ROWS), yp)
    recv("ra3")
    combine((SAF, CHIP), [(PF, block(1, 3), in_a), (RA, 3 * CHIP, all_a)], 0, ROWS)
    send("rafm0", part(SAF, CHIP, 0, ROWS), part(RAF, CHIP, 0, ROWS), ym)

    for d in (0, 3, 1, 2):
        recv("a_x%d" % d)
        to_sibling(cols_a, 1, d)
    recv("b_pp")
    to_sibling(cols_b, 0, 2)
    recv("bx_mm")
    to_sibling(cols_b, 1, 2)

    recv("rb2p")
    combine((SBF, 0), [(PF, block(0, 1), in_b), (RB2, 0, all_b)])
    send("rbf00", part(SBF, 0), part(RBF, 0), yp)
    recv("rb2m")
    combine((SBF, 3 * CHIP), [(PF, block(1, 3), in_b), (RB2, CHIP, all_b)])
    send("rbf11", part(SBF, 3 * CHIP), part(RBF, 3 * CHIP), ym)
    recv("ra2p")
    combine((SAF, 0), [(PF, block(1, 1), in_a), (RA, CHIP, all_a), (RA2, 0, all_a)], 0, ROWS)
    send("rafp0", part(SAF, 0, 0, ROWS), part(RAF, 0, 0, ROWS), yp)
    recv("ra2m")
    combine((SAF, CHIP), [(PF, block(1, 3), in_a), (RA, 3 * CHIP, all_a), (RA2, 0, all_a)], ROWS, ROWS)
    send("rafm1", part(SAF, CHIP, ROWS, ROWS), part(RAF, CHIP, ROWS, ROWS), ym)

    recv("g_rest")
    arrived(G.at[CHIP:TOKENS, 0:HALF], group_sem.at[G_IN], group_sem.at[G_OUT])
    load_w.wait()
    DH[...] = jnp.zeros(DH.shape, F32)

    def hidden_grad(i, carry):
        here = pl.ds(pl.multiple_of(i * 512, 128), 512)
        DH[...] += lax.dot_general(
            G[:, here], W[:, here], (((1,), (1,)), ((), ())), preferred_element_type=F32
        )
        return carry

    lax.fori_loop(0, D // 512, hidden_grad, 0)

    arrived(SR, group_sem.at[S_IN], group_sem.at[S_OUT])
    arrived(QR, group_sem.at[Q_IN], group_sem.at[Q_OUT])
    EC[...] = jnp.zeros(EC.shape, F32)
    gg_ref[...] = jnp.zeros(gg_ref.shape, F32)
    lane = lax.broadcasted_iota(jnp.int32, (CHIP, 128), 1)

    def chip_of(b):
        return ((y + b % 4) % 4) * 2 + (xl + b // 4) % 2

    def chunk_sums(b, carry):
        rows = pl.ds(pl.multiple_of(b * CHIP, CHIP), CHIP)
        grad = DH[rows, :]
        normed = SR[rows, :].astype(F32)
        gg_ref[...] += jnp.sum(grad * normed, axis=0, keepdims=True)
        scaled = grad.astype(BF).astype(F32) * scale
        first = jnp.sum(scaled, axis=1, keepdims=True)
        second = jnp.sum(scaled * normed, axis=1, keepdims=True)
        at = 2 * chip_of(b)
        EC[0:CHIP, :] += jnp.where(lane == at, first, 0.0) + jnp.where(lane == at + 1, second, 0.0)
        return carry

    lax.fori_loop(0, 8, chunk_sums, 0)
    ES[...] = EC[...].T[0:16, :]
    own_e = pltpu.make_async_copy(ES, ER.at[c], group_sem.at[E_IN])
    own_e.start()

    def send_e(i, carry):
        target = (t + i) % 16
        grouped(ES, ER.at[slot_at(target)], E_OUT, E_IN, (s, target))
        return carry

    lax.fori_loop(1, 16, send_e, 0)

    def deliver(src, cols):
        for core in range(2):
            grouped(
                src.at[core * ROWS : (core + 1) * ROWS, :],
                next_ref.at[:, cols],
                N_OUT,
                N_IN,
                (following, y * 4 + (1 - xl) * 2 + core),
            )

    recv("rbf00")
    recv("rbf10")
    combine(
        (SBX, 0),
        [(PF, block(0, 0), in_b), (RBF, 0, all_b), (RBF, 2 * CHIP, all_b), (XRES, 0, in_b)],
    )
    send("rbx", SBX, RBX, pair)
    recv("ra0")
    for name in ("rafp0", "rafp1", "rafm0", "rafm1"):
        recv(name)
    combine((OA, 0), [(PF, block(1, 0), in_a), (RA, 0, all_a), (RAF, 0, all_a), (RAF, CHIP, all_a)])
    deliver(OA, cols_a)

    arrived(ER, group_sem.at[E_IN], group_sem.at[E_OUT])
    EC[...] = jnp.zeros(EC.shape, F32)
    total = ER[0]
    for k in range(1, 16):
        total = total + ER[k]
    QC[0:16, :] = total * (1.0 / D)
    for b in range(8):
        EC[2 * b : 2 * b + 2, :] = QC[pl.ds(2 * chip_of(b), 2), :]
    means = EC[...].T
    QC[...] = jnp.zeros(QC.shape, F32)
    for k in range(16):
        QC[k : k + 1, :] = QR[k, 0:1, :]
    recips = QC[...].T
    for b in range(8):
        for core in range(2):
            k = b * 2 + core
            rows = pl.ds(k * ROWS, ROWS)
            mean_e = means[core * ROWS : (core + 1) * ROWS, 2 * b : 2 * b + 1]
            mean_en = means[core * ROWS : (core + 1) * ROWS, 2 * b + 1 : 2 * b + 2]
            recip = recips[0:ROWS, k : k + 1]
            scaled = DH[rows, :].astype(BF).astype(F32) * scale
            inner = scaled - mean_e - SR[rows, :].astype(F32) * mean_en
            upstream = G[rows, columns(t * WIDTH, WIDTH)].astype(F32)
            GI[rows, :] = (upstream + recip * inner).astype(BF)
            target = chip_of(b) * 2 + core
            grouped(
                GI.at[rows, :], prev_ref.at[:, columns(t * WIDTH, WIDTH)], P_OUT, P_IN, (previous, target)
            )

    recv("rbf01")
    recv("rbf11")
    recv("rbx")
    combine(
        (OB, 0),
        [(PF, block(1, 0), in_b), (RBF, CHIP, all_b), (RBF, 3 * CHIP, all_b), (RBX, 0, all_b)],
    )
    deliver(OB, cols_b)

    BHT[...] = (SR[...].astype(F32) * scale).T.astype(BF)

    def weight_grad(i, carry):
        here = pl.ds(pl.multiple_of(i * 256, 128), 256)
        W[:, here] = jnp.dot(BHT[...], G[:, here], preferred_element_type=F32).astype(BF)
        pltpu.make_async_copy(W.at[:, here], wg_ref.at[:, here], local_sem.at[6]).start()
        return carry

    lax.fori_loop(0, D // 256, weight_grad, 0)

    pltpu.make_async_copy(W, wg_ref, local_sem.at[6]).wait()
    for copy in sent:
        copy.wait_send()
    left(NX.at[:, 0 : 15 * WIDTH], group_sem.at[X_OUT], group_sem.at[X_IN])
    left(NS, group_sem.at[S_OUT], group_sem.at[S_IN])
    left(QR, group_sem.at[Q_OUT], group_sem.at[Q_IN])
    left(ER.at[0:15], group_sem.at[E_OUT], group_sem.at[E_IN])
    left(G.at[CHIP:TOKENS, 0:HALF], group_sem.at[G_OUT], group_sem.at[G_IN])
    left(GI, group_sem.at[P_OUT], group_sem.at[P_IN])
    left(next_ref, group_sem.at[N_OUT], group_sem.at[N_IN])
    arrived(prev_ref, group_sem.at[P_IN], group_sem.at[P_OUT])
    arrived(next_ref, group_sem.at[N_IN], group_sem.at[N_OUT])


def local(forward_in, grad_out, saved_in, weight, gain):
    anywhere = pl.BlockSpec(memory_space=pl.ANY)
    vmem = pl.BlockSpec(memory_space=pltpu.VMEM)
    v = pltpu.VMEM
    outs = pl.pallas_call(
        kernel,
        out_shape=(
            jax.ShapeDtypeStruct((ROWS, D), BF),
            jax.ShapeDtypeStruct((ROWS, D), BF),
            jax.ShapeDtypeStruct((WIDTH, D), BF),
            jax.ShapeDtypeStruct((1, WIDTH), F32),
        ),
        in_specs=[anywhere, anywhere, anywhere, anywhere, vmem],
        out_specs=(anywhere, anywhere, anywhere, vmem),
        scratch_shapes=[
            v((TOKENS, D), BF),
            v((WIDTH, D), BF),
            v((2 * WIDTH, HALF), BF),
            v((TOKENS, HALF), F32),
            v((TOKENS, 2 * WIDTH), BF),
            v((TOKENS, WIDTH), BF),
            v((ROWS, D), BF),
            v((ROWS, D), BF),
            v((ROWS, D), BF),
            v((ROWS, D), BF),
            v((TOKENS, WIDTH), BF),
            v((WIDTH, TOKENS), BF),
            v((TOKENS, WIDTH), F32),
            v((TOKENS, WIDTH), BF),
            v((CHIP, HALF), BF),
            v((4 * CHIP, CA), BF),
            v((4 * CHIP, CA), BF),
            v((CHIP, CA), BF),
            v((CHIP, CA), BF),
            v((2 * CHIP, CA), BF),
            v((2 * CHIP, CA), BF),
            v((2 * CHIP, CB), BF),
            v((2 * CHIP, CB), BF),
            v((4 * CHIP, CB), BF),
            v((4 * CHIP, CB), BF),
            v((CHIP, CB), BF),
            v((CHIP, CB), BF),
            v((CHIP, CA), BF),
            v((CHIP, CB), BF),
            v((128, 128), F32),
            v((8, 128), F32),
            v((16, 8, 128), F32),
            v((128, 128), F32),
            v((16, 128), F32),
            v((16, 16, 128), F32),
            pltpu.SemaphoreType.DMA((48,)),
            pltpu.SemaphoreType.DMA((48,)),
            pltpu.SemaphoreType.DMA((7,)),
            pltpu.SemaphoreType.DMA((14,)),
        ],
        compiler_params=pltpu.CompilerParams(
            collective_id=0, has_side_effects=True, vmem_limit_bytes=60 * 2**20
        ),
        cost_estimate=pl.CostEstimate(
            flops=6 * TOKENS * WIDTH * D, bytes_accessed=20 * 2**20, transcendentals=0
        ),
    )(forward_in[0], grad_out[0], saved_in[0], weight[0], gain)
    next_input, prev_grad, weight_grad, gain_grad = outs
    return next_input[None], prev_grad[None], weight_grad[None], gain_grad


def solution(mesh):
    rows = P("section", "tensor", None)
    return jax.shard_map(
        local,
        mesh=mesh,
        in_specs=(rows, rows, rows, rows, P("section", "tensor")),
        out_specs=(rows, rows, rows, P("section", "tensor")),
        check_vma=False,
    )
```

time: 349 us -> 126 us (0.36)
  waiting for transfers between devices: 217 us -> 0 us
  Pallas kernels: 0 us -> 116 us
  other arithmetic: 38.8 us -> 0 us
  matrix products: 30.5 us -> 0 us
  starting transfers between devices: 22.2 us -> 0 us
  blocking collectives: 20.4 us -> 0 us
  between operations: 13.9 us -> 0.64 us
  local copies, waits for them, and re-layouts: 3.48 us -> 9.45 us
    pallas_call x0 -> x1, Pallas kernels: none -> 116 us  [local(): pl.pallas_call(kernel, out_shape=(jax.ShapeDtypeStruct((ROWS, D), BF), ja...]
    reduce_scatter x1 -> x0, waiting for transfers between devices: 89.4 us -> none  [local(): lax.psum_scatter(jnp.dot(hidden, matrix, preferred_element_type=jnp.float...]
    all_gather x3 -> x0, waiting for transfers between devices: 70.1 us -> none  [the longest x1 41.9 us: local(): lax.all_gather(upstream, 'tensor', axis=0, tiled=True)]
    ppermute x5 -> x0, waiting for transfers between devices: 40 us -> none  [the longest x3 36.6 us: partner(): lax.ppermute(shard, axis, [(i, i ^ 1 << apart) for i in range(lax.axis_si...]
    reduce_sum x8 -> x0, other arithmetic: 36.9 us -> none  [the longest x3 26 us: normalize(): jnp.mean(shifted * shifted, axis=1, keepdims=True) + 1e-05]
    dot_general x3 -> x0, matrix products: 30.5 us -> none  [the longest x1 10.3 us: local(): jnp.dot(hidden, matrix, preferred_element_type=jnp.float32)]
    all_gather x1 -> x0, blocking collectives: 20.4 us -> none  [local(): lax.all_gather(scales, 'tensor', axis=0, tiled=True)]
    ppermute x5 -> x0, starting transfers between devices: 17 us -> none  [the longest x3 9.41 us: partner(): lax.ppermute(shard, axis, [(i, i ^ 1 << apart) for i in range(lax.axis_si...]
  transfers between devices with their start and end apart: 10 -> 0, of which waited for: 9 -> 0; matrix products, arithmetic and copies ran while one was open for 20% -> 0% of each run, Pallas kernels for 0% -> 0%
where the time goes in v1:
time: 126 us
  Pallas kernels  116 us (92%)
  local copies, waits for them, and re-layouts  9.45 us (7%)
    pallas_call x1, Pallas kernels, local(): pl.pallas_call(kernel, out_shape=(jax.ShapeDtypeStruct((ROWS, D), BF), ja...  116 us
    unnamed x6, local copies, waits for them, and re-layouts  9.45 us

profile of v1, /device:TPU:1, one launch (start us, length us, event | category | flops | bytes accessed | tf_op | source)
XLA Modules:
  0.0 126.0 jit_solution(7316366560292232272)
XLA Ops:
  0.6 115.9 %shard_map.84 = (bf16[48,6144]{1,0:T(8,128)(2,1)}, bf16[48,6144]{1,0:T(8,128)(2,1)}, bf16[384,6144]{1,0:T(8,128)(2,1)}, f32[1,384]{1,0:T(1,128)}) custom-call(bf16[48,6144]{1,0:T(8,128)(2,1)} %bitcast.11, bf16[48,6144]{1,0:T(8,128)(2,1)} %bitcast.12, bf16[48,6144]{1,0:T(8,128)(2,1)} %bitcast.13, bf16[384,6144]{1,0:T(8,128)(2,1)} %bitcast.10, ...), custom_call_target="tpu_custom_call" | custom-call | flops 10871635968 | bytes 20971520 | tf_op jit(solution)/shard_map/pallas_call | solution.py:472
  116.5 1.9 %copy.13 = bf16[1,48,6144]{2,1,0:T(8,128)(2,1)} copy(bf16[1,48,6144]{2,1,0:T(8,128)(2,1)} %bitcast.9) | data formatting | bytes 1179648
  118.4 1.9 %copy.14 = bf16[1,48,6144]{2,1,0:T(8,128)(2,1)} copy(bf16[1,48,6144]{2,1,0:T(8,128)(2,1)} %bitcast.8) | data formatting | bytes 1179648
  120.4 0.0 copy-start
  120.4 5.1 %copy.15 = bf16[1,384,6144]{2,1,0:T(8,128)(2,1)} copy(bf16[1,384,6144]{2,1,0:T(8,128)(2,1)} %bitcast.7) | data formatting | bytes 9437184
  125.4 0.0 copy-done
  125.4 0.6 copy.16
Async XLA Ops:
  120.4 5.1 %copy-start = (f32[1,384]{1,0:T(1,128)S(1)}, f32[1,384]{1,0:T(1,128)}, u32[]{:S(2)}) copy-start(f32[1,384]{1,0:T(1,128)} %get-tuple-element.19) | copy-start | bytes 4612

commit v2 on v0

v2 whole, which is shorter than its diff:
```python
import jax
import jax.numpy as jnp
from jax import lax
from jax.experimental import pallas as pl
from jax.experimental.pallas import tpu as pltpu
from jax.sharding import PartitionSpec as P

D = 6144
TOKENS = 768
ROWS = 48
CHIP = 96
WIDTH = 384
PAIRED = 2 * WIDTH
HALF = D // 2
GA = 1408
GB = HALF - GA
CA = 1280
CB = HALF - CA
SUB_A = ((0, 768), (768, 512))
SUB_B = ((0, 768), (768, 512), (1280, 512))
ORDER = (
    "first_o", "norm_s", "norm_x", "first_s", "x01", "inchip", "x03", "x12", "x02", "x13", "s11", "x10", "x11", "ap",
    "bx", "s01", "s10", "k_ax0", "am", "bp", "s02", "s12", "hidden", "dh0", "k_ax3", "bxm", "proj_a", "k_bm", "s03",
    "proj_b", "k_ax1", "ax2", "s00", "k_bxp", "rbf10_1", "s13", "rbf10_0", "rb2m_0", "rb2m_1", "ra2_0", "dh1",
    "rb2p_0", "rb2p_1", "k_bxmm", "rb2p_2", "ra3_0", "ra0_0", "dh2", "k_ax2", "k_bpp", "proj_c", "s_sib", "rbf00_0",
    "dh3", "sums", "rbf01_0", "bht", "rbf11_0", "rbx_0", "rbf01_1", "rbf00_2", "rbf10_2", "rbf00_1", "ra1_0",
    "rb2m_2", "gi", "a2_0", "a3_0", "ra2_1", "fin_b_0", "p_go", "p00", "rbf11_1", "p01", "p12", "p03", "wg2", "a1_0",
    "p11", "a2m_0", "wg0", "p10", "ra3_1", "ra1_1", "p02", "rbx_1", "a2p_0", "p13", "rbf01_2", "rbf11_2", "a2_1",
    "a3_1", "a2m_1", "fin_a_0", "rbx_2", "fin_b_1", "a1_1", "ra0_1", "a2p_1", "fin_b_2", "fin_a_1", "wg3", "wg1",
)
STRIP = 16
BF = jnp.bfloat16
F32 = jnp.float32
EPS = 1e-05
MESH = pl.DeviceIdType.MESH


def block(r, d):
    return (r * 4 + d) * CHIP


def normalize(values):
    center = jnp.mean(values, axis=1, keepdims=True)
    shifted = values - center
    recip = lax.rsqrt(jnp.mean(shifted * shifted, axis=1, keepdims=True) + EPS)
    return shifted * recip, recip


def strips(rows, body):
    def step(i, carry):
        body(pl.ds(pl.multiple_of(i * STRIP, STRIP), STRIP), i)
        return carry

    lax.fori_loop(0, rows // STRIP, step, 0)


def columns(start, width):
    return pl.ds(pl.multiple_of(start, 128), width)


def kernel(
    x_ref, g_ref, s_ref, w_ref, gain_ref,
    next_ref, prev_ref, wg_ref, gg_ref,
    G, W, WC, PF, HN, XR, XO, NX, SO, NS, SR, SF, BHT, DH, GI, GR, XRES, GS,
    SA, RA, SA2, RA2, SAF, RAF, SB2, RB2, SBF, RBF, SBX, RBX, OA, OB,
    QC, QS, QR, QF, EC, ES, ER,
    send_sem, recv_sem, local_sem, group_sem, entered,
):
    s = lax.axis_index("section")
    t = lax.axis_index("tensor")
    y, xl, c = t // 4, (t // 2) % 2, t % 2
    mirrored, following, previous = 7 - s, (s + 1) % 8, (s + 7) % 8

    def at(section, along_y, row, core):
        return (section, ((y + along_y) % 4) * 4 + row * 2 + core)

    def row(r):
        return xl if r == 0 else 1 - xl

    sib = at(s, 0, xl, 1 - c)
    yp, ym = at(s, 1, xl, c), at(s, 3, xl, c)
    pair = at(s, 0, 1 - xl, c)

    mine = c * HALF
    other = (1 - c) * HALF
    cols_a = columns(mine, GA)
    cols_b = columns(mine + GA, GB)
    own_rows = pl.ds(pl.multiple_of(c * ROWS, 16), ROWS)
    sib_rows = pl.ds(pl.multiple_of((1 - c) * ROWS, 16), ROWS)

    names = {}
    sent = []

    def send(name, src, dst, device):
        i = names.setdefault(name, (len(names), dst))[0]
        copy = pltpu.make_async_remote_copy(
            src_ref=src, dst_ref=dst, send_sem=send_sem.at[i], recv_sem=recv_sem.at[i],
            device_id=device, device_id_type=MESH,
        )
        copy.start()
        sent.append(copy)

    def arrived(ref, sem, scratch_sem):
        pltpu.make_async_remote_copy(
            src_ref=ref, dst_ref=ref, send_sem=scratch_sem, recv_sem=sem, device_id=sib, device_id_type=MESH
        ).wait_recv()

    def left(ref, sem, scratch_sem):
        pltpu.make_async_remote_copy(
            src_ref=ref, dst_ref=ref, send_sem=sem, recv_sem=scratch_sem, device_id=sib, device_id_type=MESH
        ).wait_send()

    def recv(*wanted):
        for name in wanted:
            i, landing = names[name]
            arrived(landing, recv_sem.at[i], send_sem.at[i])

    E_IN, E_OUT, P_IN, P_OUT, N_IN, N_OUT = range(6)

    def grouped(src, dst, out, into, device):
        pltpu.make_async_remote_copy(
            src_ref=src, dst_ref=dst, send_sem=group_sem.at[out], recv_sem=group_sem.at[into],
            device_id=device, device_id_type=MESH,
        ).start()

    barrier = pltpu.get_barrier_semaphore()
    gateways = [at(section, 0, xl, c) for section in (mirrored, previous, following)]
    comrades = [at(s, e, row(r), core) for e in (1, 3, 0, 2) for r in range(2) for core in (c, 1 - c)]
    comrades = [comrade for i, comrade in enumerate(comrades) if i != 8]
    for friend in comrades + gateways:
        pl.semaphore_signal(barrier, inc=1, device_id=friend, device_id_type=MESH)

    load_x = pltpu.make_async_copy(x_ref, XO, local_sem.at[0])
    load_g = pltpu.make_async_copy(g_ref, G.at[own_rows, :], local_sem.at[1])
    load_s = pltpu.make_async_copy(s_ref, SO, local_sem.at[2])
    load_w = pltpu.make_async_copy(w_ref, W, local_sem.at[3])
    weight_rows = pl.ds(pl.multiple_of(c * WIDTH, 128), WIDTH)
    load_wc = pltpu.make_async_copy(w_ref.at[:, columns(mine, HALF)], WC.at[weight_rows, :], local_sem.at[4])
    load_xres = pltpu.make_async_copy(x_ref.at[:, columns(mine, HALF)], XRES.at[own_rows, :], local_sem.at[5])
    for load in (load_x, load_g, load_s, load_wc, load_xres, load_w):
        load.start()
    scale = gain_ref[...].astype(F32)
    GS[:, columns(c * WIDTH, WIDTH)] = jnp.broadcast_to(scale, (8, WIDTH))

    pl.semaphore_wait(barrier, 18)

    for gateway, entry in zip(gateways, (0, 2, 1)):
        pl.semaphore_signal(entered.at[entry], inc=1, device_id=gateway, device_id_type=MESH)

    def own(cols, r=0, d=0, first=0, rows=CHIP):
        return G.at[block(r, d) + first : block(r, d) + first + rows, cols]

    def near(cols, rows, r, d):
        return G.at[pl.ds(pl.multiple_of(block(r, d) + rows.start, 16), ROWS), cols]

    def from_here(e, r):
        return r * 4 + (4 - e) % 4

    tasks = {}

    def task(run):
        tasks[run.__name__] = run
        return run

    def first_step(part, a, b):
        send("b_x" + part, b[0], near(cols_b, b[1], 1, 0), pair)
        send("a_p" + part, a[0], near(cols_a, a[1], 0, 3), yp)
        send("a_m" + part, a[0], near(cols_a, a[1], 0, 1), ym)
        send("b_p" + part, b[0], near(cols_b, b[1], 0, 3), yp)
        send("b_m" + part, b[0], near(cols_b, b[1], 0, 1), ym)
        send("a_x0" + part, a[0], near(cols_a, a[1], 1, 0), pair)

    @task
    def first_o():
        send("g_half", g_ref.at[:, columns(other, HALF)], G.at[own_rows, columns(other, HALF)], sib)
        first_step("o", (g_ref.at[:, cols_a], own_rows), (g_ref.at[:, cols_b], own_rows))

    @task
    def first_s():
        recv("g_half")
        first_step("s", (G.at[sib_rows, cols_a], sib_rows), (G.at[sib_rows, cols_b], sib_rows))

    @task
    def inchip():
        send("gain", GS.at[:, columns(c * WIDTH, WIDTH)], GS.at[:, columns(c * WIDTH, WIDTH)], sib)
        send("w_half", w_ref.at[:, columns(other, HALF)], WC.at[weight_rows, :], sib)
        send("x_half", x_ref.at[:, columns(other, HALF)], XRES.at[own_rows, :], sib)
        send("g_rest", g_ref.at[:, columns(mine, HALF)], G.at[own_rows, columns(mine, HALF)], sib)

    @task
    def norm_x():
        load_x.wait()

        def body(rows, i):
            NX[rows, :] = normalize(XO[rows, :].astype(F32))[0].astype(BF)

        strips(ROWS, body)

    def features(e, r):
        return columns((((y + e) % 4) * 2 + row(r)) * PAIRED, PAIRED)

    def x_task(e, r):
        def run():
            send("x%d%d" % (r, e), NX.at[:, features(e, r)], XR.at[from_here(e, r)], at(s, e, row(r), c))

        tasks["x%d%d" % (r, e)] = run

    @task
    def norm_s():
        load_s.wait()
        QC[...] = jnp.zeros(QC.shape, F32)

        def body(rows, i):
            normed, recip = normalize(SO[rows, :].astype(F32))
            NS[rows, :] = normed.astype(BF)
            QC[rows, :] = jnp.broadcast_to(recip, (STRIP, 128))

        strips(ROWS, body)
        QS[...] = QC[...].T[0:8, :]
        pl.semaphore_wait(entered.at[0], 1)

    def s_task(e, r):
        def run():
            target = at(mirrored, e, row(r), c)
            send("s%d%d" % (r, e), NS.at[:, features(e, r)], SR.at[from_here(e, r)], target)
            send("q%d%d" % (r, e), QS, QR.at[from_here(e, r)], target)

        tasks["s%d%d" % (r, e)] = run

    for e in range(4):
        for r in range(2):
            s_task(e, r)
            if (e, r) != (0, 0):
                x_task(e, r)

    def share(name, cols, r, d):
        ref = own(cols, r, d)
        send(name, ref, ref, sib)

    @task
    def bx():
        recv("b_xo", "b_xs")
        send("bx_p", own(cols_b, 1, 0), own(cols_b, 1, 3), yp)
        send("bx_m", own(cols_b, 1, 0), own(cols_b, 1, 1), ym)
        share("Gb10", cols_b, 1, 0)

    @task
    def ap():
        recv("a_po", "a_ps")
        send("a_pp", own(cols_a, 0, 3, 0, ROWS), own(cols_a, 0, 2, 0, ROWS), yp)
        send("a_x3", own(cols_a, 0, 3), own(cols_a, 1, 3), pair)
        share("Ga03", cols_a, 0, 3)

    @task
    def am():
        recv("a_mo", "a_ms")
        send("a_mm", own(cols_a, 0, 1, ROWS, ROWS), own(cols_a, 0, 2, ROWS, ROWS), ym)
        send("a_x1", own(cols_a, 0, 1), own(cols_a, 1, 1), pair)
        share("Ga01", cols_a, 0, 1)

    @task
    def bp():
        recv("b_po", "b_ps")
        send("b_pp", own(cols_b, 0, 3), own(cols_b, 0, 2), yp)
        share("Gb03", cols_b, 0, 3)

    @task
    def bxm():
        recv("bx_m")
        send("bx_mm", own(cols_b, 1, 1), own(cols_b, 1, 2), ym)
        share("Gb11", cols_b, 1, 1)

    @task
    def ax2():
        recv("a_pp", "a_mm")
        send("a_x2", own(cols_a, 0, 2), own(cols_a, 1, 2), pair)
        share("Ga02", cols_a, 0, 2)

    def keep_task(name, wanted, cols, r, d):
        def run():
            recv(*wanted)
            share("G%s%d%d" % ("a" if cols is cols_a else "b", r, d), cols, r, d)

        tasks[name] = run

    keep_task("k_bm", ("b_mo", "b_ms"), cols_b, 0, 1)
    keep_task("k_bxp", ("bx_p",), cols_b, 1, 3)
    keep_task("k_ax0", ("a_x0o", "a_x0s"), cols_a, 1, 0)
    keep_task("k_ax3", ("a_x3",), cols_a, 1, 3)
    keep_task("k_ax1", ("a_x1",), cols_a, 1, 1)
    keep_task("k_bpp", ("b_pp",), cols_b, 0, 2)
    keep_task("k_bxmm", ("bx_mm",), cols_b, 1, 2)
    keep_task("k_ax2", ("a_x2",), cols_a, 1, 2)

    @task
    def hidden():
        recv("gain")
        both = GS[0:1, :]
        for d in (0, 3, 1, 2):
            for r in range(2):
                if (d, r) == (0, 0):
                    values = NX[:, features(0, 0)]
                else:
                    recv("x%d%d" % (r, (4 - d) % 4))
                    values = XR[r * 4 + d]
                HN[r * 4 + d, own_rows, :] = (values.astype(F32) * both).astype(BF)
        send("hid", HN.at[:, own_rows, :], HN.at[:, own_rows, :], sib)

    def project(first, chips, start, width, store):
        def tile(i, carry):
            here = pl.multiple_of(i * 256, 256)
            there = pl.ds(pl.multiple_of(start + here, 256), 256)
            store(
                pl.ds(here, 256),
                there,
                jnp.dot(
                    HN[first : first + chips].reshape(chips * CHIP, PAIRED),
                    WC[:, there],
                    preferred_element_type=F32,
                ),
            )
            return carry

        lax.fori_loop(0, width // 256, tile, 0)

    @task
    def proj_a():
        pl.semaphore_wait(entered.at[2], 1)
        load_wc.wait()
        load_xres.wait()
        recv("hid", "w_half", "x_half")

        def store(here, there, value):
            SA[0:CHIP, here] = (value[0:CHIP] + XRES[:, here].astype(F32)).astype(BF)
            SA[CHIP : 4 * CHIP, here] = value[CHIP : 4 * CHIP].astype(BF)

        project(0, 4, 0, CA, store)

    @task
    def proj_b():
        def store(here, there, value):
            PF[:, there] = value

        project(0, 8, CA, CB, store)

    @task
    def proj_c():
        def store(here, there, value):
            PF[4 * CHIP : 8 * CHIP, here] = value

        project(4, 4, 0, CA, store)

    def combine(dst, terms, width, first=0, rows=CHIP):
        def body(strip, i):
            total = None
            for ref, base, start in terms:
                here = pl.ds(pl.multiple_of(base + first + i * STRIP, STRIP), STRIP)
                value = ref[here, start : start + width].astype(F32)
                total = value if total is None else total + value
            ref, base, start = dst
            ref[pl.ds(pl.multiple_of(base + first + i * STRIP, STRIP), STRIP), start : start + width] = total.astype(BF)

        strips(rows, body)

    def deliver(src, start, width, offset):
        for core in range(2):
            grouped(
                src.at[core * ROWS : (core + 1) * ROWS, start : start + width],
                next_ref.at[:, columns(mine + offset + start, width)],
                N_OUT,
                N_IN,
                at(following, 0, 1 - xl, core),
            )

    def reduce_a(k):
        a, w = SUB_A[k]

        def pass_on(name, src, dst, first, rows, device):
            send(
                "%s_%d" % (name, k), src.at[first : first + rows, a : a + w], dst.at[first : first + rows, a : a + w], device
            )

        def cross(d):
            def run():
                pass_on("ra%d" % d, SA, RA, d * CHIP, CHIP, pair)

            tasks["ra%d_%d" % (d, k)] = run

        for d in range(4):
            cross(d)

        def a2():
            recv("ra2_%d" % k)
            combine((SA2, 0, a), [(PF, block(1, 2), a), (RA, 2 * CHIP, a)], w)
            pass_on("ra2p", SA2, RA2, 0, ROWS, yp)
            pass_on("ra2m", SA2, RA2, ROWS, ROWS, ym)

        def a1():
            recv("ra1_%d" % k)
            combine((SAF, 0, a), [(PF, block(1, 1), a), (RA, CHIP, a)], w, ROWS, ROWS)
            pass_on("rafp1", SAF, RAF, ROWS, ROWS, yp)

        def a3():
            recv("ra3_%d" % k)
            combine((SAF, CHIP, a), [(PF, block(1, 3), a), (RA, 3 * CHIP, a)], w, 0, ROWS)
            pass_on("rafm0", SAF, RAF, CHIP, ROWS, ym)

        def a2p():
            recv("ra2p_%d" % k)
            combine((SAF, 0, a), [(PF, block(1, 1), a), (RA, CHIP, a), (RA2, 0, a)], w, 0, ROWS)
            pass_on("rafp0", SAF, RAF, 0, ROWS, yp)

        def a2m():
            recv("ra2m_%d" % k)
            combine((SAF, CHIP, a), [(PF, block(1, 3), a), (RA, 3 * CHIP, a), (RA2, 0, a)], w, ROWS, ROWS)
            pass_on("rafm1", SAF, RAF, CHIP + ROWS, ROWS, ym)

        def fin_a():
            for name in ("ra0", "rafp0", "rafp1", "rafm0", "rafm1"):
                recv("%s_%d" % (name, k))
            combine((OA, 0, a), [(PF, block(1, 0), a), (RA, 0, a), (RAF, 0, a), (RAF, CHIP, a)], w)
            deliver(OA, a, w, 0)

        for run in (a2, a1, a3, a2p, a2m, fin_a):
            tasks["%s_%d" % (run.__name__, k)] = run

    def reduce_b(k):
        a, w = SUB_B[k]

        def hand(name, src, dst, first, device, terms):
            combine((src, first, a), terms, w)
            send(
                "%s_%d" % (name, k), src.at[first : first + CHIP, a : a + w], dst.at[first : first + CHIP, a : a + w], device
            )

        def rb2p():
            hand("rb2p", SB2, RB2, 0, yp, [(PF, block(0, 2), CA + a)])

        def rb2m():
            hand("rb2m", SB2, RB2, CHIP, ym, [(PF, block(1, 2), CA + a)])

        def rbf01():
            hand("rbf01", SBF, RBF, CHIP, yp, [(PF, block(1, 1), CA + a)])

        def rbf10():
            hand("rbf10", SBF, RBF, 2 * CHIP, ym, [(PF, block(0, 3), CA + a)])

        def rbf00():
            recv("rb2p_%d" % k)
            hand("rbf00", SBF, RBF, 0, yp, [(PF, block(0, 1), CA + a), (RB2, 0, a)])

        def rbf11():
            recv("rb2m_%d" % k)
            hand("rbf11", SBF, RBF, 3 * CHIP, ym, [(PF, block(1, 3), CA + a), (RB2, CHIP, a)])

        def rbx():
            recv("rbf00_%d" % k, "rbf10_%d" % k)
            hand(
                "rbx", SBX, RBX, 0, pair,
                [(PF, block(0, 0), CA + a), (RBF, 0, a), (RBF, 2 * CHIP, a), (XRES, 0, CA + a)],
            )

        def fin_b():
            recv("rbf01_%d" % k, "rbf11_%d" % k, "rbx_%d" % k)
            combine((OB, 0, a), [(PF, block(1, 0), CA + a), (RBF, CHIP, a), (RBF, 3 * CHIP, a), (RBX, 0, a)], w)
            deliver(OB, a, w, CA)

        for run in (rb2p, rb2m, rbf01, rbf10, rbf00, rbf11, rbx, fin_b):
            tasks["%s_%d" % (run.__name__, k)] = run

    for k in range(len(SUB_A)):
        reduce_a(k)
    for k in range(len(SUB_B)):
        reduce_b(k)

    def dh_task(i, blocks, wanted):
        def run():
            recv(*wanted)
            if i == 0:
                load_g.wait()
                load_w.wait()
            first, second = (pl.ds(block(r, d), CHIP) for r, d in blocks)
            DH[first, :] = jnp.zeros((CHIP, WIDTH), F32)
            DH[second, :] = jnp.zeros((CHIP, WIDTH), F32)

            def step(j, carry):
                here = pl.ds(pl.multiple_of(j * 1024, 1024), 1024)
                part = lax.dot_general(
                    jnp.concatenate([G[first, here], G[second, here]], axis=0),
                    W[:, here],
                    (((1,), (1,)), ((), ())),
                    preferred_element_type=F32,
                )
                DH[first, :] += part[0:CHIP]
                DH[second, :] += part[CHIP : 2 * CHIP]
                return carry

            lax.fori_loop(0, D // 1024, step, 0)

        tasks["dh%d" % i] = run

    dh_task(0, ((0, 0), (1, 0)), ("g_rest", "Ga10", "Gb10"))
    dh_task(1, ((0, 1), (0, 3)), ("Ga03", "Ga01", "Gb03", "Gb01"))
    dh_task(2, ((1, 1), (1, 3)), ("Ga13", "Ga11", "Gb13", "Gb11"))
    dh_task(3, ((0, 2), (1, 2)), ("Ga02", "Ga12", "Gb02", "Gb12"))

    def local_copy(i, src, dst):
        copy = pltpu.make_async_copy(src, dst, local_sem.at[i])
        copy.start()
        return copy

    kept = {}

    @task
    def s_sib():
        for e in (1, 3, 2, 0):
            for r in range(2):
                recv("s%d%d" % (r, e), "q%d%d" % (r, e))
        send("s_sib", SR.at[:, :, columns((1 - c) * WIDTH, WIDTH)], SF.at[:, own_rows, :], sib)
        send("q_sib", QR, QF.at[:, c], sib)
        kept["s"] = local_copy(7, SR.at[:, :, columns(c * WIDTH, WIDTH)], SF.at[:, own_rows, :])
        kept["q"] = local_copy(8, QR, QF.at[:, c])

    def chip_of(b):
        return ((y + b % 4) % 4) * 2 + (xl + b // 4) % 2

    @task
    def sums():
        recv("s_sib", "q_sib")
        kept["s"].wait()
        kept["q"].wait()
        EC[...] = jnp.zeros(EC.shape, F32)
        gg_ref[...] = jnp.zeros(gg_ref.shape, F32)
        lane = lax.broadcasted_iota(jnp.int32, (CHIP, 128), 1)

        def chunk(b, carry):
            grad = DH[pl.ds(pl.multiple_of(b * CHIP, CHIP), CHIP), :]
            normed = SF[b].astype(F32)
            gg_ref[...] += jnp.sum(grad * normed, axis=0, keepdims=True)
            scaled = grad.astype(BF).astype(F32) * scale
            first = jnp.sum(scaled, axis=1, keepdims=True)
            second = jnp.sum(scaled * normed, axis=1, keepdims=True)
            place = 2 * chip_of(b)
            EC[0:CHIP, :] += jnp.where(lane == place, first, 0.0) + jnp.where(lane == place + 1, second, 0.0)
            return carry

        lax.fori_loop(0, 8, chunk, 0)
        ES[...] = EC[...].T[0:16, :]
        pltpu.make_async_copy(ES, ER.at[c], group_sem.at[E_IN]).start()
        for e in (2, 1, 3, 0):
            for r in range(2):
                grouped(ES, ER.at[from_here(e, r) * 2 + c], E_OUT, E_IN, at(s, e, row(r), 1 - c))
                if (e, r) != (0, 0):
                    grouped(ES, ER.at[from_here(e, r) * 2 + c], E_OUT, E_IN, at(s, e, row(r), c))

    @task
    def gi():
        arrived(ER, group_sem.at[E_IN], group_sem.at[E_OUT])
        total = ER[0]
        for k in range(1, 16):
            total = total + ER[k]
        QC[0:16, :] = total * (1.0 / D)
        EC[...] = jnp.zeros(EC.shape, F32)
        for b in range(8):
            EC[2 * b : 2 * b + 2, :] = QC[pl.ds(2 * chip_of(b), 2), :]
        means = EC[...].T
        QC[...] = jnp.zeros(QC.shape, F32)
        for b in range(8):
            for core in range(2):
                QC[b * 2 + core : b * 2 + core + 1, :] = QF[b, core, 0:1, :]
        recips = QC[...].T
        for b in range(8):
            for core in range(2):
                k = b * 2 + core
                part = slice(core * ROWS, (core + 1) * ROWS)
                rows = slice(k * ROWS, (k + 1) * ROWS)
                mean_e = means[part, 2 * b : 2 * b + 1]
                mean_en = means[part, 2 * b + 1 : 2 * b + 2]
                recip = recips[0:ROWS, k : k + 1]
                scaled = DH[rows, :].astype(BF).astype(F32) * scale
                inner = scaled - mean_e - SF[b, part, :].astype(F32) * mean_en
                upstream = G[rows, columns(t * WIDTH, WIDTH)].astype(F32)
                GI[b, part, :] = (upstream + recip * inner).astype(BF)
        here = columns(c * WIDTH, WIDTH)
        send("p_sib", GI.at[:, sib_rows, :], GR.at[:, :, here], sib)
        kept["p"] = local_copy(9, GI.at[:, own_rows, :], GR.at[:, :, here])

    @task
    def p_go():
        pl.semaphore_wait(entered.at[1], 1)
        kept["p"].wait()
        recv("p_sib")

    def p_task(e, r):
        def run():
            grouped(GR.at[r * 4 + e], prev_ref.at[:, features(0, 0)], P_OUT, P_IN, at(previous, e, row(r), c))

        tasks["p%d%d" % (r, e)] = run

    for e in range(4):
        for r in range(2):
            p_task(e, r)

    @task
    def bht():
        BHT[...] = (SF[...].reshape(TOKENS, WIDTH).astype(F32) * scale).T.astype(BF)

    def wg_task(i):
        def run():
            def step(j, carry):
                here = pl.ds(pl.multiple_of(j * 256, 256), 256)
                W[:, here] = jnp.dot(BHT[...], G[:, here], preferred_element_type=F32).astype(BF)
                pltpu.make_async_copy(W.at[:, here], wg_ref.at[:, here], local_sem.at[6]).start()
                return carry

            lax.fori_loop(i * 6, (i + 1) * 6, step, 0)

        tasks["wg%d" % i] = run

    for i in range(4):
        wg_task(i)

    for name in ORDER:
        tasks[name]()

    pltpu.make_async_copy(W, wg_ref, local_sem.at[6]).wait()
    for copy in sent:
        copy.wait_send()
    left(ER.at[0:15], group_sem.at[E_OUT], group_sem.at[E_IN])
    left(next_ref, group_sem.at[N_OUT], group_sem.at[N_IN])
    left(prev_ref, group_sem.at[P_OUT], group_sem.at[P_IN])
    arrived(prev_ref, group_sem.at[P_IN], group_sem.at[P_OUT])
    arrived(next_ref, group_sem.at[N_IN], group_sem.at[N_OUT])


PARTS = 6


def hand_over(next_in, prev_in, wg_in, gg_in, next_out, prev_out, wg_out, gg_out, near_next, near_prev, near_wg, sems):
    gg_out[...] = gg_in[...]
    rows = WIDTH // PARTS
    moves = [(wg_in.at[i], near_wg.at[i], wg_out.at[i]) for i in (pl.ds(k * rows, rows) for k in range(PARTS))]
    moves += [(next_in, near_next, next_out), (prev_in, near_prev, prev_out)]
    inward = [pltpu.make_async_copy(src, via, sems.at[0, i]) for i, (src, via, dst) in enumerate(moves)]
    outward = [pltpu.make_async_copy(via, dst, sems.at[1, i]) for i, (src, via, dst) in enumerate(moves)]
    for copy in inward:
        copy.start()
    for before, after in zip(inward, outward):
        before.wait()
        after.start()
    for copy in outward:
        copy.wait()


def local(forward_in, grad_out, saved_in, weight, gain):
    anywhere = pl.BlockSpec(memory_space=pl.ANY)
    vmem = pl.BlockSpec(memory_space=pltpu.VMEM)
    v = pltpu.VMEM
    out_shape = (
        jax.ShapeDtypeStruct((ROWS, D), BF),
        jax.ShapeDtypeStruct((ROWS, D), BF),
        jax.ShapeDtypeStruct((WIDTH, D), BF),
        jax.ShapeDtypeStruct((1, WIDTH), F32),
    )
    raw = pl.pallas_call(
        kernel,
        out_shape=out_shape,
        in_specs=[anywhere, anywhere, anywhere, anywhere, vmem],
        out_specs=(anywhere, anywhere, anywhere, vmem),
        scratch_shapes=[
            v((TOKENS, D), BF),
            v((WIDTH, D), BF),
            v((PAIRED, HALF), BF),
            v((TOKENS, HALF), F32),
            v((8, CHIP, PAIRED), BF),
            v((8, ROWS, PAIRED), BF),
            v((ROWS, D), BF),
            v((ROWS, D), BF),
            v((ROWS, D), BF),
            v((ROWS, D), BF),
            v((8, ROWS, PAIRED), BF),
            v((8, CHIP, WIDTH), BF),
            v((WIDTH, TOKENS), BF),
            v((TOKENS, WIDTH), F32),
            v((8, CHIP, WIDTH), BF),
            v((8, ROWS, PAIRED), BF),
            v((CHIP, HALF), BF),
            v((8, PAIRED), F32),
            v((4 * CHIP, CA), BF),
            v((4 * CHIP, CA), BF),
            v((CHIP, CA), BF),
            v((CHIP, CA), BF),
            v((2 * CHIP, CA), BF),
            v((2 * CHIP, CA), BF),
            v((2 * CHIP, CB), BF),
            v((2 * CHIP, CB), BF),
            v((4 * CHIP, CB), BF),
            v((4 * CHIP, CB), BF),
            v((CHIP, CB), BF),
            v((CHIP, CB), BF),
            v((CHIP, CA), BF),
            v((CHIP, CB), BF),
            v((128, 128), F32),
            v((8, 128), F32),
            v((8, 8, 128), F32),
            v((8, 2, 8, 128), F32),
            v((128, 128), F32),
            v((16, 128), F32),
            v((16, 16, 128), F32),
            pltpu.SemaphoreType.DMA((128,)),
            pltpu.SemaphoreType.DMA((128,)),
            pltpu.SemaphoreType.DMA((10,)),
            pltpu.SemaphoreType.DMA((6,)),
            pltpu.SemaphoreType.REGULAR((3,)),
        ],
        compiler_params=pltpu.CompilerParams(
            collective_id=0, has_side_effects=True, vmem_limit_bytes=60 * 2**20
        ),
        cost_estimate=pl.CostEstimate(
            flops=6 * TOKENS * WIDTH * D, bytes_accessed=20 * 2**20, transcendentals=0
        ),
    )(forward_in[0], grad_out[0], saved_in[0], weight[0], gain)
    next_input, prev_grad, weight_grad, gain_grad = pl.pallas_call(
        hand_over,
        out_shape=out_shape,
        in_specs=[pl.BlockSpec(memory_space=pltpu.HBM)] * 3 + [vmem],
        out_specs=(anywhere, anywhere, anywhere, vmem),
        scratch_shapes=[
            v((ROWS, D), BF),
            v((ROWS, D), BF),
            v((WIDTH, D), BF),
            pltpu.SemaphoreType.DMA((2, PARTS + 2)),
        ],
        cost_estimate=pl.CostEstimate(flops=0, bytes_accessed=12 * 2**20, transcendentals=0),
    )(*raw)
    return next_input[None], prev_grad[None], weight_grad[None], gain_grad


def solution(mesh):
    rows = P("section", "tensor", None)
    return jax.shard_map(
        local,
        mesh=mesh,
        in_specs=(rows, rows, rows, rows, P("section", "tensor")),
        out_specs=(rows, rows, rows, P("section", "tensor")),
        check_vma=False,
    )
```

time: 349 us -> 112 us (0.32)
  waiting for transfers between devices: 217 us -> 0 us
  Pallas kernels: 0 us -> 111 us
  other arithmetic: 38.8 us -> 0 us
  matrix products: 30.5 us -> 0 us
  starting transfers between devices: 22.2 us -> 0 us
  blocking collectives: 20.4 us -> 0 us
  between operations: 13.9 us -> 0.64 us
    pallas_call x0 -> x2, Pallas kernels: none -> 111 us  [the longest x1 105 us: local(): pl.pallas_call(kernel, out_shape=out_shape, in_specs=[anywhere, anywhere,...]
    reduce_scatter x1 -> x0, waiting for transfers between devices: 89.4 us -> none  [local(): lax.psum_scatter(jnp.dot(hidden, matrix, preferred_element_type=jnp.float...]
    all_gather x3 -> x0, waiting for transfers between devices: 70.1 us -> none  [the longest x1 41.9 us: local(): lax.all_gather(upstream, 'tensor', axis=0, tiled=True)]
    ppermute x5 -> x0, waiting for transfers between devices: 40 us -> none  [the longest x3 36.6 us: partner(): lax.ppermute(shard, axis, [(i, i ^ 1 << apart) for i in range(lax.axis_si...]
    reduce_sum x8 -> x0, other arithmetic: 36.9 us -> none  [the longest x3 26 us: normalize(): jnp.mean(shifted * shifted, axis=1, keepdims=True) + 1e-05]
    dot_general x3 -> x0, matrix products: 30.5 us -> none  [the longest x1 10.3 us: local(): jnp.dot(hidden, matrix, preferred_element_type=jnp.float32)]
    all_gather x1 -> x0, blocking collectives: 20.4 us -> none  [local(): lax.all_gather(scales, 'tensor', axis=0, tiled=True)]
    ppermute x5 -> x0, starting transfers between devices: 17 us -> none  [the longest x3 9.41 us: partner(): lax.ppermute(shard, axis, [(i, i ^ 1 << apart) for i in range(lax.axis_si...]
  transfers between devices with their start and end apart: 10 -> 0, of which waited for: 9 -> 0; matrix products, arithmetic and copies ran while one was open for 20% -> 0% of each run, Pallas kernels for 0% -> 0%
where the time goes in v2:
time: 112 us
  Pallas kernels  111 us (99%)
    pallas_call x1, Pallas kernels, local(): pl.pallas_call(kernel, out_shape=out_shape, in_specs=[anywhere, anywhere,...  105 us
    pallas_call x1, Pallas kernels, local(): pl.pallas_call(hand_over, out_shape=out_shape, in_specs=[pl.BlockSpec(mem...  6.37 us

profile of v2, /device:TPU:1, one launch (start us, length us, event | category | flops | bytes accessed | tf_op | source)
XLA Modules:
  0.0 111.5 jit_solution(7023431269044005115)
XLA Ops:
  0.6 104.5 %shard_map.84 = (bf16[48,6144]{1,0:T(8,128)(2,1)}, bf16[48,6144]{1,0:T(8,128)(2,1)}, bf16[384,6144]{1,0:T(8,128)(2,1)}, f32[1,384]{1,0:T(1,128)}) custom-call(bf16[48,6144]{1,0:T(8,128)(2,1)} %bitcast.9, bf16[48,6144]{1,0:T(8,128)(2,1)} %bitcast.10, bf16[48,6144]{1,0:T(8,128)(2,1)} %bitcast.11, bf16[384,6144]{1,0:T(8,128)(2,1)} %bitcast.7, ...), custom_call_target="tpu_custom_call" | custom-call | flops 10871635968 | bytes 20971520 | tf_op jit(solution)/shard_map/pallas_call | solution.py:665
  105.1 6.4 %shard_map.85 = (bf16[48,6144]{1,0:T(8,128)(2,1)}, bf16[48,6144]{1,0:T(8,128)(2,1)}, bf16[384,6144]{1,0:T(8,128)(2,1)}, f32[1,384]{1,0:T(1,128)}) custom-call(bf16[48,6144]{1,0:T(8,128)(2,1)} %get-tuple-element.12.next_in, bf16[48,6144]{1,0:T(8,128)(2,1)} %get-tuple-element.13.prev_in, bf16[384,6144]{1,0:T(8,128)(2,1)} %get-tuple-element.14.wg_in, ...), custom_call_target="tpu_custom_call" | custom-call | bytes 12582912 | tf_op jit(solution)/shard_map/pallas_call | solution.py:723

commit v3 on v2

--- a/solution.py
+++ b/solution.py
@@ -19,16 +19,20 @@
 SUB_A = ((0, 768), (768, 512))
 SUB_B = ((0, 768), (768, 512), (1280, 512))
 ORDER = (
-    "first_o", "norm_s", "norm_x", "first_s", "x01", "inchip", "x03", "x12", "x02", "x13", "s11", "x10", "x11", "ap",
-    "bx", "s01", "s10", "k_ax0", "am", "bp", "s02", "s12", "hidden", "dh0", "k_ax3", "bxm", "proj_a", "k_bm", "s03",
-    "proj_b", "k_ax1", "ax2", "s00", "k_bxp", "rbf10_1", "s13", "rbf10_0", "rb2m_0", "rb2m_1", "ra2_0", "dh1",
-    "rb2p_0", "rb2p_1", "k_bxmm", "rb2p_2", "ra3_0", "ra0_0", "dh2", "k_ax2", "k_bpp", "proj_c", "s_sib", "rbf00_0",
-    "dh3", "sums", "rbf01_0", "bht", "rbf11_0", "rbx_0", "rbf01_1", "rbf00_2", "rbf10_2", "rbf00_1", "ra1_0",
-    "rb2m_2", "gi", "a2_0", "a3_0", "ra2_1", "fin_b_0", "p_go", "p00", "rbf11_1", "p01", "p12", "p03", "wg2", "a1_0",
-    "p11", "a2m_0", "wg0", "p10", "ra3_1", "ra1_1", "p02", "rbx_1", "a2p_0", "p13", "rbf01_2", "rbf11_2", "a2_1",
-    "a3_1", "a2m_1", "fin_a_0", "rbx_2", "fin_b_1", "a1_1", "ra0_1", "a2p_1", "fin_b_2", "fin_a_1", "wg3", "wg1",
+    6, 0, 9, 7, 1, 23, 19, 2, 17, 25,
+    8, 3, 21, 10, 11, 15, 26, 4, 13, 12,
+    5, 22, 28, 40, 27, 34, 24, 32, 29, 30,
+    41, 18, 20, 42, 64, 31, 14, 36, 75, 16,
+    35, 43, 37, 89, 46, 33, 67, 47, 65, 88,
+    66, 68, 39, 80, 45, 81, 38, 56, 83, 90,
+    92, 91, 93, 94, 72, 84, 69, 70, 104, 48,
+    95, 97, 55, 50, 99, 103, 102, 82, 96, 58,
+    71, 44, 49, 106, 86, 52, 51, 57, 73, 54,
+    101, 59, 76, 105, 85, 53, 100, 98, 61, 60,
+    62, 77, 107, 78, 74, 87, 63, 79, 108,
 )
 STRIP = 16
+ROUNDS = 5
 BF = jnp.bfloat16
 F32 = jnp.float32
 EPS = 1e-05
@@ -61,10 +65,10 @@
 def kernel(
     x_ref, g_ref, s_ref, w_ref, gain_ref,
     next_ref, prev_ref, wg_ref, gg_ref,
-    G, W, WC, PF, HN, XR, XO, NX, SO, NS, SR, SF, BHT, DH, GI, GR, XRES, GS,
+    G, W, WC, PF, HN, XR, XO, NX, SO, NS, SR, SF, BHT, DH, GI, XRES, GS,
     SA, RA, SA2, RA2, SAF, RAF, SB2, RB2, SBF, RBF, SBX, RBX, OA, OB,
-    QC, QS, QR, QF, EC, ES, ER,
-    send_sem, recv_sem, local_sem, group_sem, entered,
+    QC, QS, QR, QF, EC, ES, ER, MT, RT,
+    send_sem, recv_sem, local_sem, group_sem, heard,
 ):
     s = lax.axis_index("section")
     t = lax.axis_index("tensor")
@@ -124,10 +128,9 @@
         ).start()
 
     barrier = pltpu.get_barrier_semaphore()
-    gateways = [at(section, 0, xl, c) for section in (mirrored, previous, following)]
-    comrades = [at(s, e, row(r), core) for e in (1, 3, 0, 2) for r in range(2) for core in (c, 1 - c)]
-    comrades = [comrade for i, comrade in enumerate(comrades) if i != 8]
-    for friend in comrades + gateways:
+    across = at(s + 1 - 2 * (s % 2), 0, 1 - xl, c)
+    nearest = [sib, yp, ym, pair, across, at((s + 2) % 8, 0, xl, c), at((s + 6) % 8, 0, xl, c)]
+    for friend in nearest:
         pl.semaphore_signal(barrier, inc=1, device_id=friend, device_id_type=MESH)
 
     load_x = pltpu.make_async_copy(x_ref, XO, local_sem.at[0])
@@ -142,10 +145,7 @@
     scale = gain_ref[...].astype(F32)
     GS[:, columns(c * WIDTH, WIDTH)] = jnp.broadcast_to(scale, (8, WIDTH))
 
-    pl.semaphore_wait(barrier, 18)
-
-    for gateway, entry in zip(gateways, (0, 2, 1)):
-        pl.semaphore_signal(entered.at[entry], inc=1, device_id=gateway, device_id_type=MESH)
+    pl.semaphore_wait(barrier, len(nearest))
 
     def own(cols, r=0, d=0, first=0, rows=CHIP):
         return G.at[block(r, d) + first : block(r, d) + first + rows, cols]
@@ -156,29 +156,42 @@
     def from_here(e, r):
         return r * 4 + (4 - e) % 4
 
-    tasks = {}
+    tasks = []
 
     def task(run):
-        tasks[run.__name__] = run
+        tasks.append(run)
         return run
 
+    def round_task(i):
+        def run():
+            if i > 1:
+                pl.semaphore_wait(heard.at[i - 2], len(nearest))
+            if i <= ROUNDS:
+                for friend in nearest:
+                    pl.semaphore_signal(heard.at[i - 1], inc=1, device_id=friend, device_id_type=MESH)
+
+        tasks.append(run)
+
+    for i in range(1, ROUNDS + 2):
+        round_task(i)
+
     def first_step(part, a, b):
-        send("b_x" + part, b[0], near(cols_b, b[1], 1, 0), pair)
-        send("a_p" + part, a[0], near(cols_a, a[1], 0, 3), yp)
-        send("a_m" + part, a[0], near(cols_a, a[1], 0, 1), ym)
-        send("b_p" + part, b[0], near(cols_b, b[1], 0, 3), yp)
-        send("b_m" + part, b[0], near(cols_b, b[1], 0, 1), ym)
-        send("a_x0" + part, a[0], near(cols_a, a[1], 1, 0), pair)
+        send(("b_x", part), b[0], near(cols_b, b[1], 1, 0), pair)
+        send(("a_p", part), a[0], near(cols_a, a[1], 0, 3), yp)
+        send(("a_m", part), a[0], near(cols_a, a[1], 0, 1), ym)
+        send(("b_p", part), b[0], near(cols_b, b[1], 0, 3), yp)
+        send(("b_m", part), b[0], near(cols_b, b[1], 0, 1), ym)
+        send(("a_x0", part), a[0], near(cols_a, a[1], 1, 0), pair)
 
     @task
     def first_o():
         send("g_half", g_ref.at[:, columns(other, HALF)], G.at[own_rows, columns(other, HALF)], sib)
-        first_step("o", (g_ref.at[:, cols_a], own_rows), (g_ref.at[:, cols_b], own_rows))
+        first_step(0, (g_ref.at[:, cols_a], own_rows), (g_ref.at[:, cols_b], own_rows))
 
     @task
     def first_s():
         recv("g_half")
-        first_step("s", (G.at[sib_rows, cols_a], sib_rows), (G.at[sib_rows, cols_b], sib_rows))
+        first_step(1, (G.at[sib_rows, cols_a], sib_rows), (G.at[sib_rows, cols_b], sib_rows))
 
     @task
     def inchip():
@@ -201,9 +214,9 @@
 
     def x_task(e, r):
         def run():
-            send("x%d%d" % (r, e), NX.at[:, features(e, r)], XR.at[from_here(e, r)], at(s, e, row(r), c))
-
-        tasks["x%d%d" % (r, e)] = run
+            send(("x", r, e), NX.at[:, features(e, r)], XR.at[from_here(e, r)], at(s, e, row(r), c))
+
+        tasks.append(run)
 
     @task
     def norm_s():
@@ -217,15 +230,14 @@
 
         strips(ROWS, body)
         QS[...] = QC[...].T[0:8, :]
-        pl.semaphore_wait(entered.at[0], 1)
 
     def s_task(e, r):
         def run():
             target = at(mirrored, e, row(r), c)
-            send("s%d%d" % (r, e), NS.at[:, features(e, r)], SR.at[from_here(e, r)], target)
-            send("q%d%d" % (r, e), QS, QR.at[from_here(e, r)], target)
-
-        tasks["s%d%d" % (r, e)] = run
+            send(("s", r, e), NS.at[:, features(e, r)], SR.at[from_here(e, r)], target)
+            send(("q", r, e), QS, QR.at[from_here(e, r)], target)
+
+        tasks.append(run)
 
     for e in range(4):
         for r in range(2):
@@ -233,67 +245,72 @@
             if (e, r) != (0, 0):
                 x_task(e, r)
 
-    def share(name, cols, r, d):
+    def share(cols, r, d):
         ref = own(cols, r, d)
-        send(name, ref, ref, sib)
+        send((cols is cols_a, r, d), ref, ref, sib)
+
+    def halves(name):
+        return (name, 0), (name, 1)
 
     @task
     def bx():
-        recv("b_xo", "b_xs")
+        recv(*halves("b_x"))
         send("bx_p", own(cols_b, 1, 0), own(cols_b, 1, 3), yp)
         send("bx_m", own(cols_b, 1, 0), own(cols_b, 1, 1), ym)
-        share("Gb10", cols_b, 1, 0)
+        share(cols_b, 1, 0)
 
     @task
     def ap():
-        recv("a_po", "a_ps")
+        recv(*halves("a_p"))
         send("a_pp", own(cols_a, 0, 3, 0, ROWS), own(cols_a, 0, 2, 0, ROWS), yp)
         send("a_x3", own(cols_a, 0, 3), own(cols_a, 1, 3), pair)
-        share("Ga03", cols_a, 0, 3)
+        share(cols_a, 0, 3)
 
     @task
     def am():
-        recv("a_mo", "a_ms")
+        recv(*halves("a_m"))
         send("a_mm", own(cols_a, 0, 1, ROWS, ROWS), own(cols_a, 0, 2, ROWS, ROWS), ym)
         send("a_x1", own(cols_a, 0, 1), own(cols_a, 1, 1), pair)
-        share("Ga01", cols_a, 0, 1)
+        share(cols_a, 0, 1)
 
     @task
     def bp():
-        recv("b_po", "b_ps")
+        recv(*halves("b_p"))
         send("b_pp", own(cols_b, 0, 3), own(cols_b, 0, 2), yp)
-        share("Gb03", cols_b, 0, 3)
+        share(cols_b, 0, 3)
 
     @task
     def bxm():
         recv("bx_m")
         send("bx_mm", own(cols_b, 1, 1), own(cols_b, 1, 2), ym)
-        share("Gb11", cols_b, 1, 1)
+        share(cols_b, 1, 1)
 
     @task
     def ax2():
         recv("a_pp", "a_mm")
         send("a_x2", own(cols_a, 0, 2), own(cols_a, 1, 2), pair)
-        share("Ga02", cols_a, 0, 2)
-
-    def keep_task(name, wanted, cols, r, d):
+        share(cols_a, 0, 2)
+
+    def keep_task(wanted, cols, r, d):
         def run():
             recv(*wanted)
-            share("G%s%d%d" % ("a" if cols is cols_a else "b", r, d), cols, r, d)
-
-        tasks[name] = run
-
-    keep_task("k_bm", ("b_mo", "b_ms"), cols_b, 0, 1)
-    keep_task("k_bxp", ("bx_p",), cols_b, 1, 3)
-    keep_task("k_ax0", ("a_x0o", "a_x0s"), cols_a, 1, 0)
-    keep_task("k_ax3", ("a_x3",), cols_a, 1, 3)
-    keep_task("k_ax1", ("a_x1",), cols_a, 1, 1)
-    keep_task("k_bpp", ("b_pp",), cols_b, 0, 2)
-    keep_task("k_bxmm", ("bx_mm",), cols_b, 1, 2)
-    keep_task("k_ax2", ("a_x2",), cols_a, 1, 2)
+            share(cols, r, d)
+
+        tasks.append(run)
+
+    keep_task(halves("b_m"), cols_b, 0, 1)
+    keep_task(("bx_p",), cols_b, 1, 3)
+    keep_task(halves("a_x0"), cols_a, 1, 0)
+    keep_task(("a_x3",), cols_a, 1, 3)
+    keep_task(("a_x1",), cols_a, 1, 1)
+    keep_task(("b_pp",), cols_b, 0, 2)
+    keep_task(("bx_mm",), cols_b, 1, 2)
+    keep_task(("a_x2",), cols_a, 1, 2)
 
     @task
     def hidden():
+        load_g.wait()
+        load_w.wait()
         recv("gain")
         both = GS[0:1, :]
         for d in (0, 3, 1, 2):
@@ -301,7 +318,7 @@
                 if (d, r) == (0, 0):
                     values = NX[:, features(0, 0)]
                 else:
-                    recv("x%d%d" % (r, (4 - d) % 4))
+                    recv(("x", r, (4 - d) % 4))
                     values = XR[r * 4 + d]
                 HN[r * 4 + d, own_rows, :] = (values.astype(F32) * both).astype(BF)
         send("hid", HN.at[:, own_rows, :], HN.at[:, own_rows, :], sib)
@@ -325,7 +342,6 @@
 
     @task
     def proj_a():
-        pl.semaphore_wait(entered.at[2], 1)
         load_wc.wait()
         load_xres.wait()
         recv("hid", "w_half", "x_half")
@@ -377,52 +393,51 @@
 
         def pass_on(name, src, dst, first, rows, device):
             send(
-                "%s_%d" % (name, k), src.at[first : first + rows, a : a + w], dst.at[first : first + rows, a : a + w], device
+                (name, k), src.at[first : first + rows, a : a + w], dst.at[first : first + rows, a : a + w], device
             )
 
         def cross(d):
             def run():
-                pass_on("ra%d" % d, SA, RA, d * CHIP, CHIP, pair)
-
-            tasks["ra%d_%d" % (d, k)] = run
+                pass_on(d, SA, RA, d * CHIP, CHIP, pair)
+
+            tasks.append(run)
 
         for d in range(4):
             cross(d)
 
         def a2():
-            recv("ra2_%d" % k)
+            recv((2, k))
             combine((SA2, 0, a), [(PF, block(1, 2), a), (RA, 2 * CHIP, a)], w)
             pass_on("ra2p", SA2, RA2, 0, ROWS, yp)
             pass_on("ra2m", SA2, RA2, ROWS, ROWS, ym)
 
         def a1():
-            recv("ra1_%d" % k)
+            recv((1, k))
             combine((SAF, 0, a), [(PF, block(1, 1), a), (RA, CHIP, a)], w, ROWS, ROWS)
             pass_on("rafp1", SAF, RAF, ROWS, ROWS, yp)
 
         def a3():
-            recv("ra3_%d" % k)
+            recv((3, k))
             combine((SAF, CHIP, a), [(PF, block(1, 3), a), (RA, 3 * CHIP, a)], w, 0, ROWS)
             pass_on("rafm0", SAF, RAF, CHIP, ROWS, ym)
 
         def a2p():
-            recv("ra2p_%d" % k)
+            recv(("ra2p", k))
             combine((SAF, 0, a), [(PF, block(1, 1), a), (RA, CHIP, a), (RA2, 0, a)], w, 0, ROWS)
             pass_on("rafp0", SAF, RAF, 0, ROWS, yp)
 
         def a2m():
-            recv("ra2m_%d" % k)
+            recv(("ra2m", k))
             combine((SAF, CHIP, a), [(PF, block(1, 3), a), (RA, 3 * CHIP, a), (RA2, 0, a)], w, ROWS, ROWS)
             pass_on("rafm1", SAF, RAF, CHIP + ROWS, ROWS, ym)
 
         def fin_a():
-            for name in ("ra0", "rafp0", "rafp1", "rafm0", "rafm1"):
-                recv("%s_%d" % (name, k))
+            for name in (0, "rafp0", "rafp1", "rafm0", "rafm1"):
+                recv((name, k))
             combine((OA, 0, a), [(PF, block(1, 0), a), (RA, 0, a), (RAF, 0, a), (RAF, CHIP, a)], w)
             deliver(OA, a, w, 0)
 
-        for run in (a2, a1, a3, a2p, a2m, fin_a):
-            tasks["%s_%d" % (run.__name__, k)] = run
+        tasks.extend((a2, a1, a3, a2p, a2m, fin_a))
 
     def reduce_b(k):
         a, w = SUB_B[k]
@@ -430,7 +445,7 @@
         def hand(name, src, dst, first, device, terms):
             combine((src, first, a), terms, w)
             send(
-                "%s_%d" % (name, k), src.at[first : first + CHIP, a : a + w], dst.at[first : first + CHIP, a : a + w], device
+                (name, k), src.at[first : first + CHIP, a : a + w], dst.at[first : first + CHIP, a : a + w], device
             )
 
         def rb2p():
@@ -446,39 +461,35 @@
             hand("rbf10", SBF, RBF, 2 * CHIP, ym, [(PF, block(0, 3), CA + a)])
 
         def rbf00():
-            recv("rb2p_%d" % k)
+            recv(("rb2p", k))
             hand("rbf00", SBF, RBF, 0, yp, [(PF, block(0, 1), CA + a), (RB2, 0, a)])
 
         def rbf11():
-            recv("rb2m_%d" % k)
+            recv(("rb2m", k))
             hand("rbf11", SBF, RBF, 3 * CHIP, ym, [(PF, block(1, 3), CA + a), (RB2, CHIP, a)])
 
         def rbx():
-            recv("rbf00_%d" % k, "rbf10_%d" % k)
+            recv(("rbf00", k), ("rbf10", k))
             hand(
                 "rbx", SBX, RBX, 0, pair,
                 [(PF, block(0, 0), CA + a), (RBF, 0, a), (RBF, 2 * CHIP, a), (XRES, 0, CA + a)],
             )
 
         def fin_b():
-            recv("rbf01_%d" % k, "rbf11_%d" % k, "rbx_%d" % k)
+            recv(("rbf01", k), ("rbf11", k), ("rbx", k))
             combine((OB, 0, a), [(PF, block(1, 0), CA + a), (RBF, CHIP, a), (RBF, 3 * CHIP, a), (RBX, 0, a)], w)
             deliver(OB, a, w, CA)
 
-        for run in (rb2p, rb2m, rbf01, rbf10, rbf00, rbf11, rbx, fin_b):
-            tasks["%s_%d" % (run.__name__, k)] = run
+        tasks.extend((rb2p, rb2m, rbf01, rbf10, rbf00, rbf11, rbx, fin_b))
 
     for k in range(len(SUB_A)):
         reduce_a(k)
     for k in range(len(SUB_B)):
         reduce_b(k)
 
-    def dh_task(i, blocks, wanted):
+    def dh_task(blocks, wanted):
         def run():
             recv(*wanted)
-            if i == 0:
-                load_g.wait()
-                load_w.wait()
             first, second = (pl.ds(block(r, d), CHIP) for r, d in blocks)
             DH[first, :] = jnp.zeros((CHIP, WIDTH), F32)
             DH[second, :] = jnp.zeros((CHIP, WIDTH), F32)
@@ -497,12 +508,12 @@
 
             lax.fori_loop(0, D // 1024, step, 0)
 
-        tasks["dh%d" % i] = run
-
-    dh_task(0, ((0, 0), (1, 0)), ("g_rest", "Ga10", "Gb10"))
-    dh_task(1, ((0, 1), (0, 3)), ("Ga03", "Ga01", "Gb03", "Gb01"))
-    dh_task(2, ((1, 1), (1, 3)), ("Ga13", "Ga11", "Gb13", "Gb11"))
-    dh_task(3, ((0, 2), (1, 2)), ("Ga02", "Ga12", "Gb02", "Gb12"))
+        tasks.append(run)
+
+    dh_task(((0, 0), (1, 0)), ("g_rest", (True, 1, 0), (False, 1, 0)))
+    dh_task(((0, 1), (0, 3)), ((True, 0, 3), (True, 0, 1), (False, 0, 3), (False, 0, 1)))
+    dh_task(((1, 1), (1, 3)), ((True, 1, 3), (True, 1, 1), (False, 1, 3), (False, 1, 1)))
+    dh_task(((0, 2), (1, 2)), ((True, 0, 2), (True, 1, 2), (False, 0, 2), (False, 1, 2)))
 
     def local_copy(i, src, dst):
         copy = pltpu.make_async_copy(src, dst, local_sem.at[i])
@@ -515,7 +526,7 @@
     def s_sib():
         for e in (1, 3, 2, 0):
             for r in range(2):
-                recv("s%d%d" % (r, e), "q%d%d" % (r, e))
+                recv(("s", r, e), ("q", r, e))
         send("s_sib", SR.at[:, :, columns((1 - c) * WIDTH, WIDTH)], SF.at[:, own_rows, :], sib)
         send("q_sib", QR, QF.at[:, c], sib)
         kept["s"] = local_copy(7, SR.at[:, :, columns(c * WIDTH, WIDTH)], SF.at[:, own_rows, :])
@@ -524,17 +535,10 @@
     def chip_of(b):
         return ((y + b % 4) % 4) * 2 + (xl + b // 4) % 2
 
-    @task
-    def sums():
-        recv("s_sib", "q_sib")
-        kept["s"].wait()
-        kept["q"].wait()
-        EC[...] = jnp.zeros(EC.shape, F32)
-        gg_ref[...] = jnp.zeros(gg_ref.shape, F32)
+    def add_sums(blocks):
         lane = lax.broadcasted_iota(jnp.int32, (CHIP, 128), 1)
-
-        def chunk(b, carry):
-            grad = DH[pl.ds(pl.multiple_of(b * CHIP, CHIP), CHIP), :]
+        for b in blocks:
+            grad = DH[b * CHIP : (b + 1) * CHIP, :]
             normed = SF[b].astype(F32)
             gg_ref[...] += jnp.sum(grad * normed, axis=0, keepdims=True)
             scaled = grad.astype(BF).astype(F32) * scale
@@ -542,9 +546,19 @@
             second = jnp.sum(scaled * normed, axis=1, keepdims=True)
             place = 2 * chip_of(b)
             EC[0:CHIP, :] += jnp.where(lane == place, first, 0.0) + jnp.where(lane == place + 1, second, 0.0)
-            return carry
-
-        lax.fori_loop(0, 8, chunk, 0)
+
+    @task
+    def sums_a():
+        recv("s_sib", "q_sib")
+        kept["s"].wait()
+        kept["q"].wait()
+        EC[...] = jnp.zeros(EC.shape, F32)
+        gg_ref[...] = jnp.zeros(gg_ref.shape, F32)
+        add_sums((0, 4, 1, 3, 5, 7))
+
+    @task
+    def sums_b():
+        add_sums((2, 6))
         ES[...] = EC[...].T[0:16, :]
         pltpu.make_async_copy(ES, ER.at[c], group_sem.at[E_IN]).start()
         for e in (2, 1, 3, 0):
@@ -563,39 +577,36 @@
         EC[...] = jnp.zeros(EC.shape, F32)
         for b in range(8):
             EC[2 * b : 2 * b + 2, :] = QC[pl.ds(2 * chip_of(b), 2), :]
-        means = EC[...].T
+        MT[...] = EC[...].T
         QC[...] = jnp.zeros(QC.shape, F32)
         for b in range(8):
             for core in range(2):
                 QC[b * 2 + core : b * 2 + core + 1, :] = QF[b, core, 0:1, :]
-        recips = QC[...].T
-        for b in range(8):
+        RT[...] = QC[...].T
+
+    def p_task(e, r):
+        def run():
+            b = r * 4 + e
             for core in range(2):
                 k = b * 2 + core
                 part = slice(core * ROWS, (core + 1) * ROWS)
                 rows = slice(k * ROWS, (k + 1) * ROWS)
-                mean_e = means[part, 2 * b : 2 * b + 1]
-                mean_en = means[part, 2 * b + 1 : 2 * b + 2]
-                recip = recips[0:ROWS, k : k + 1]
+                mean_e = MT[part, 2 * b : 2 * b + 1]
+                mean_en = MT[part, 2 * b + 1 : 2 * b + 2]
+                recip = RT[0:ROWS, k : k + 1]
                 scaled = DH[rows, :].astype(BF).astype(F32) * scale
                 inner = scaled - mean_e - SF[b, part, :].astype(F32) * mean_en
                 upstream = G[rows, columns(t * WIDTH, WIDTH)].astype(F32)
                 GI[b, part, :] = (upstream + recip * inner).astype(BF)
-        here = columns(c * WIDTH, WIDTH)
-        send("p_sib", GI.at[:, sib_rows, :], GR.at[:, :, here], sib)
-        kept["p"] = local_copy(9, GI.at[:, own_rows, :], GR.at[:, :, here])
-
-    @task
-    def p_go():
-        pl.semaphore_wait(entered.at[1], 1)
-        kept["p"].wait()
-        recv("p_sib")
-
-    def p_task(e, r):
-        def run():
-            grouped(GR.at[r * 4 + e], prev_ref.at[:, features(0, 0)], P_OUT, P_IN, at(previous, e, row(r), c))
-
-        tasks["p%d%d" % (r, e)] = run
+                grouped(
+                    GI.at[b, part, :],
+                    prev_ref.at[:, columns(t * WIDTH, WIDTH)],
+                    P_OUT,
+                    P_IN,
+                    at(previous, e, row(r), core),
+                )
+
+        tasks.append(run)
 
     for e in range(4):
         for r in range(2):
@@ -615,13 +626,13 @@
 
             lax.fori_loop(i * 6, (i + 1) * 6, step, 0)
 
-        tasks["wg%d" % i] = run
+        tasks.append(run)
 
     for i in range(4):
         wg_task(i)
 
-    for name in ORDER:
-        tasks[name]()
+    for i in ORDER:
+        tasks[i]()
 
     pltpu.make_async_copy(W, wg_ref, local_sem.at[6]).wait()
     for copy in sent:
@@ -633,7 +644,7 @@
     arrived(next_ref, group_sem.at[N_IN], group_sem.at[N_OUT])
 
 
-PARTS = 6
+PARTS = 2
 
 
 def hand_over(next_in, prev_in, wg_in, gg_in, next_out, prev_out, wg_out, gg_out, near_next, near_prev, near_wg, sems):
@@ -683,7 +694,6 @@
             v((WIDTH, TOKENS), BF),
             v((TOKENS, WIDTH), F32),
             v((8, CHIP, WIDTH), BF),
-            v((8, ROWS, PAIRED), BF),
             v((CHIP, HALF), BF),
             v((8, PAIRED), F32),
             v((4 * CHIP, CA), BF),
@@ -707,11 +717,13 @@
             v((128, 128), F32),
             v((16, 128), F32),
             v((16, 16, 128), F32),
+            v((128, 128), F32),
+            v((128, 128), F32),
             pltpu.SemaphoreType.DMA((128,)),
             pltpu.SemaphoreType.DMA((128,)),
-            pltpu.SemaphoreType.DMA((10,)),
+            pltpu.SemaphoreType.DMA((9,)),
             pltpu.SemaphoreType.DMA((6,)),
-            pltpu.SemaphoreType.REGULAR((3,)),
+            pltpu.SemaphoreType.REGULAR((ROUNDS,)),
         ],
         compiler_params=pltpu.CompilerParams(
             collective_id=0, has_side_effects=True, vmem_limit_bytes=60 * 2**20

time: 112 us -> 107 us (0.955)
  Pallas kernels: 111 us -> 106 us
    pallas_call x1, Pallas kernels: 105 us -> 101 us  [local(): pl.pallas_call(kernel, out_shape=out_shape, in_specs=[anywhere, anywhere,...]
where the time goes in v3:
time: 107 us
  Pallas kernels  106 us (99%)
    pallas_call x1, Pallas kernels, local(): pl.pallas_call(kernel, out_shape=out_shape, in_specs=[anywhere, anywhere,...  101 us
    pallas_call x1, Pallas kernels, local(): pl.pallas_call(hand_over, out_shape=out_shape, in_specs=[pl.BlockSpec(mem...  5.5 us

profile of v3, /device:TPU:1, one launch (start us, length us, event | category | flops | bytes accessed | tf_op | source)
XLA Modules:
  0.0 107.0 jit_solution(6162294955330149147)
XLA Ops:
  0.6 100.9 %shard_map.84 = (bf16[48,6144]{1,0:T(8,128)(2,1)}, bf16[48,6144]{1,0:T(8,128)(2,1)}, bf16[384,6144]{1,0:T(8,128)(2,1)}, f32[1,384]{1,0:T(1,128)}) custom-call(bf16[48,6144]{1,0:T(8,128)(2,1)} %bitcast.9, bf16[48,6144]{1,0:T(8,128)(2,1)} %bitcast.10, bf16[48,6144]{1,0:T(8,128)(2,1)} %bitcast.11, bf16[384,6144]{1,0:T(8,128)(2,1)} %bitcast.7, ...), custom_call_target="tpu_custom_call" | custom-call | flops 10871635968 | bytes 20971520 | tf_op jit(solution)/shard_map/pallas_call | solution.py:676
  101.5 5.5 %shard_map.85 = (bf16[48,6144]{1,0:T(8,128)(2,1)}, bf16[48,6144]{1,0:T(8,128)(2,1)}, bf16[384,6144]{1,0:T(8,128)(2,1)}, f32[1,384]{1,0:T(1,128)}) custom-call(bf16[48,6144]{1,0:T(8,128)(2,1)} %get-tuple-element.12.next_in, bf16[48,6144]{1,0:T(8,128)(2,1)} %get-tuple-element.13.prev_in, bf16[384,6144]{1,0:T(8,128)(2,1)} %get-tuple-element.14.wg_in, ...), custom_call_target="tpu_custom_call" | custom-call | bytes 12582912 | tf_op jit(solution)/shard_map/pallas_call | solution.py:735

commit v4 on v3

--- a/solution.py
+++ b/solution.py
@@ -16,20 +16,21 @@
 GB = HALF - GA
 CA = 1280
 CB = HALF - CA
-SUB_A = ((0, 768), (768, 512))
+SUB_A = ((0, 512), (512, 512), (1024, 256))
 SUB_B = ((0, 768), (768, 512), (1280, 512))
 ORDER = (
-    6, 0, 9, 7, 1, 23, 19, 2, 17, 25,
-    8, 3, 21, 10, 11, 15, 26, 4, 13, 12,
-    5, 22, 28, 40, 27, 34, 24, 32, 29, 30,
-    41, 18, 20, 42, 64, 31, 14, 36, 75, 16,
-    35, 43, 37, 89, 46, 33, 67, 47, 65, 88,
-    66, 68, 39, 80, 45, 81, 38, 56, 83, 90,
-    92, 91, 93, 94, 72, 84, 69, 70, 104, 48,
-    95, 97, 55, 50, 99, 103, 102, 82, 96, 58,
-    71, 44, 49, 106, 86, 52, 51, 57, 73, 54,
-    101, 59, 76, 105, 85, 53, 100, 98, 61, 60,
-    62, 77, 107, 78, 74, 87, 63, 79, 108,
+    6, 0, 9, 23, 1, 7, 8, 2, 19, 21,
+    17, 3, 25, 10, 15, 4, 18, 26, 20, 13,
+    27, 22, 34, 11, 28, 40, 29, 41, 30, 42,
+    82, 75, 66, 5, 32, 12, 14, 35, 43, 31,
+    99, 33, 36, 57, 24, 74, 85, 56, 98, 83,
+    16, 38, 55, 65, 86, 77, 39, 100, 78, 37,
+    84, 46, 102, 76, 88, 87, 79, 101, 80, 103,
+    104, 90, 60, 54, 89, 114, 58, 81, 67, 59,
+    93, 91, 47, 105, 107, 69, 62, 94, 106, 113,
+    68, 45, 61, 109, 48, 108, 95, 92, 112, 96,
+    70, 72, 63, 44, 111, 110, 117, 49, 51, 50,
+    71, 116, 52, 64, 115, 97, 73, 53, 118,
 )
 STRIP = 16
 ROUNDS = 5
@@ -620,8 +621,7 @@
         def run():
             def step(j, carry):
                 here = pl.ds(pl.multiple_of(j * 256, 256), 256)
-                W[:, here] = jnp.dot(BHT[...], G[:, here], preferred_element_type=F32).astype(BF)
-                pltpu.make_async_copy(W.at[:, here], wg_ref.at[:, here], local_sem.at[6]).start()
+                wg_ref[:, here] = jnp.dot(BHT[...], G[:, here], preferred_element_type=F32).astype(BF)
                 return carry
 
             lax.fori_loop(i * 6, (i + 1) * 6, step, 0)
@@ -634,7 +634,6 @@
     for i in ORDER:
         tasks[i]()
 
-    pltpu.make_async_copy(W, wg_ref, local_sem.at[6]).wait()
     for copy in sent:
         copy.wait_send()
     left(ER.at[0:15], group_sem.at[E_OUT], group_sem.at[E_IN])
@@ -642,25 +641,6 @@
     left(prev_ref, group_sem.at[P_OUT], group_sem.at[P_IN])
     arrived(prev_ref, group_sem.at[P_IN], group_sem.at[P_OUT])
     arrived(next_ref, group_sem.at[N_IN], group_sem.at[N_OUT])
-
-
-PARTS = 2
-
-
-def hand_over(next_in, prev_in, wg_in, gg_in, next_out, prev_out, wg_out, gg_out, near_next, near_prev, near_wg, sems):
-    gg_out[...] = gg_in[...]
-    rows = WIDTH // PARTS
-    moves = [(wg_in.at[i], near_wg.at[i], wg_out.at[i]) for i in (pl.ds(k * rows, rows) for k in range(PARTS))]
-    moves += [(next_in, near_next, next_out), (prev_in, near_prev, prev_out)]
-    inward = [pltpu.make_async_copy(src, via, sems.at[0, i]) for i, (src, via, dst) in enumerate(moves)]
-    outward = [pltpu.make_async_copy(via, dst, sems.at[1, i]) for i, (src, via, dst) in enumerate(moves)]
-    for copy in inward:
-        copy.start()
-    for before, after in zip(inward, outward):
-        before.wait()
-        after.start()
-    for copy in outward:
-        copy.wait()
 
 
 def local(forward_in, grad_out, saved_in, weight, gain):
@@ -673,11 +653,11 @@
         jax.ShapeDtypeStruct((WIDTH, D), BF),
         jax.ShapeDtypeStruct((1, WIDTH), F32),
     )
-    raw = pl.pallas_call(
+    next_input, prev_grad, weight_grad, gain_grad = pl.pallas_call(
         kernel,
-        out_shape=out_shape,
+        out_shape=tuple(v(out.shape, out.dtype) for out in out_shape),
         in_specs=[anywhere, anywhere, anywhere, anywhere, vmem],
-        out_specs=(anywhere, anywhere, anywhere, vmem),
+        out_specs=(vmem,) * 4,
         scratch_shapes=[
             v((TOKENS, D), BF),
             v((WIDTH, D), BF),
@@ -726,25 +706,12 @@
             pltpu.SemaphoreType.REGULAR((ROUNDS,)),
         ],
         compiler_params=pltpu.CompilerParams(
-            collective_id=0, has_side_effects=True, vmem_limit_bytes=60 * 2**20
+            collective_id=0, has_side_effects=True, vmem_limit_bytes=54 * 2**20
         ),
         cost_estimate=pl.CostEstimate(
             flops=6 * TOKENS * WIDTH * D, bytes_accessed=20 * 2**20, transcendentals=0
         ),
     )(forward_in[0], grad_out[0], saved_in[0], weight[0], gain)
-    next_input, prev_grad, weight_grad, gain_grad = pl.pallas_call(
-        hand_over,
-        out_shape=out_shape,
-        in_specs=[pl.BlockSpec(memory_space=pltpu.HBM)] * 3 + [vmem],
-        out_specs=(anywhere, anywhere, anywhere, vmem),
-        scratch_shapes=[
-            v((ROWS, D), BF),
-            v((ROWS, D), BF),
-            v((WIDTH, D), BF),
-            pltpu.SemaphoreType.DMA((2, PARTS + 2)),
-        ],
-        cost_estimate=pl.CostEstimate(flops=0, bytes_accessed=12 * 2**20, transcendentals=0),
-    )(*raw)
     return next_input[None], prev_grad[None], weight_grad[None], gain_grad
 
 

time: 107 us -> 105 us (0.981)
  Pallas kernels: 106 us -> 100 us
  local copies, waits for them, and re-layouts: 0 us -> 4.38 us
    pallas_call x2 -> x1, Pallas kernels: 106 us -> 100 us  [local(): pl.pallas_call(kernel, out_shape=tuple((v(out.shape, out.dtype) for out i...]
    unnamed x0 -> x4, local copies, waits for them, and re-layouts: none -> 4.38 us
where the time goes in v4:
time: 105 us
  Pallas kernels  100 us (95%)
  local copies, waits for them, and re-layouts  4.38 us (4%)
    pallas_call x1, Pallas kernels, local(): pl.pallas_call(kernel, out_shape=tuple((v(out.shape, out.dtype) for out i...  100 us
    unnamed x4, local copies, waits for them, and re-layouts  4.38 us

profile of v4, /device:TPU:1, one launch (start us, length us, event | category | flops | bytes accessed | tf_op | source)
XLA Modules:
  0.0 105.0 jit_solution(12790851781303682129)
XLA Ops:
  0.6 100.0 %shard_map.84 = (bf16[48,6144]{1,0:T(8,128)(2,1)S(1)}, bf16[48,6144]{1,0:T(8,128)(2,1)S(1)}, bf16[384,6144]{1,0:T(8,128)(2,1)S(1)}, f32[1,384]{1,0:T(1,128)S(1)}) custom-call(bf16[48,6144]{1,0:T(8,128)(2,1)} %bitcast.11, bf16[48,6144]{1,0:T(8,128)(2,1)} %bitcast.12, bf16[48,6144]{1,0:T(8,128)(2,1)} %bitcast.13, bf16[384,6144]{1,0:T(8,128)(2,1)} %bitcast.10, ...), custom_call_target="tpu_custom_call" | custom-call | flops 10871635968 | bytes 20971520 | tf_op jit(solution)/shard_map/pallas_call | solution.py:656
  100.6 0.8 copy.13
  101.4 0.8 copy.14
  102.3 0.6 copy.16
  102.8 2.2 %copy.15 = bf16[1,384,6144]{2,1,0:T(8,128)(2,1)} copy(bf16[1,384,6144]{2,1,0:T(8,128)(2,1)S(1)} %bitcast.7) | data formatting | bytes 9437184

commit v5 on v4

--- a/solution.py
+++ b/solution.py
@@ -17,20 +17,20 @@
 CA = 1280
 CB = HALF - CA
 SUB_A = ((0, 512), (512, 512), (1024, 256))
-SUB_B = ((0, 768), (768, 512), (1280, 512))
+SUB_B = ((0, 1024), (1024, 512), (1536, 256))
 ORDER = (
-    6, 0, 9, 23, 1, 7, 8, 2, 19, 21,
-    17, 3, 25, 10, 15, 4, 18, 26, 20, 13,
-    27, 22, 34, 11, 28, 40, 29, 41, 30, 42,
-    82, 75, 66, 5, 32, 12, 14, 35, 43, 31,
-    99, 33, 36, 57, 24, 74, 85, 56, 98, 83,
-    16, 38, 55, 65, 86, 77, 39, 100, 78, 37,
-    84, 46, 102, 76, 88, 87, 79, 101, 80, 103,
-    104, 90, 60, 54, 89, 114, 58, 81, 67, 59,
-    93, 91, 47, 105, 107, 69, 62, 94, 106, 113,
-    68, 45, 61, 109, 48, 108, 95, 92, 112, 96,
-    70, 72, 63, 44, 111, 110, 117, 49, 51, 50,
-    71, 116, 52, 64, 115, 97, 73, 53, 118,
+    6, 0, 9, 23, 1, 7, 10, 8, 19, 2,
+    21, 17, 13, 25, 3, 15, 26, 28, 20, 40,
+    4, 11, 32, 34, 22, 24, 27, 41, 12, 29,
+    5, 33, 42, 45, 30, 74, 75, 16, 31, 18,
+    43, 98, 14, 46, 47, 35, 36, 99, 38, 77,
+    78, 100, 79, 49, 66, 56, 37, 76, 48, 39,
+    102, 93, 68, 80, 101, 103, 104, 58, 82, 85,
+    55, 81, 65, 90, 51, 91, 50, 105, 67, 110,
+    109, 57, 52, 113, 114, 106, 94, 107, 69, 70,
+    71, 83, 72, 111, 86, 44, 64, 59, 60, 54,
+    117, 61, 53, 62, 108, 88, 84, 95, 87, 73,
+    63, 96, 92, 112, 118, 89, 97, 115, 116,
 )
 STRIP = 16
 ROUNDS = 5

time: 105 us -> 104 us (level)
  no operation moved by 1% of the time
where the time goes in v5:
time: 104 us
  Pallas kernels  99.2 us (95%)
  local copies, waits for them, and re-layouts  4.38 us (4%)
    pallas_call x1, Pallas kernels, local(): pl.pallas_call(kernel, out_shape=tuple((v(out.shape, out.dtype) for out i...  99.2 us
    unnamed x4, local copies, waits for them, and re-layouts  4.38 us

profile of v5, /device:TPU:1, one launch (start us, length us, event | category | flops | bytes accessed | tf_op | source)
XLA Modules:
  0.0 104.2 jit_solution(17015435582315571855)
XLA Ops:
  0.6 99.2 %shard_map.84 = (bf16[48,6144]{1,0:T(8,128)(2,1)S(1)}, bf16[48,6144]{1,0:T(8,128)(2,1)S(1)}, bf16[384,6144]{1,0:T(8,128)(2,1)S(1)}, f32[1,384]{1,0:T(1,128)S(1)}) custom-call(bf16[48,6144]{1,0:T(8,128)(2,1)} %bitcast.11, bf16[48,6144]{1,0:T(8,128)(2,1)} %bitcast.12, bf16[48,6144]{1,0:T(8,128)(2,1)} %bitcast.13, bf16[384,6144]{1,0:T(8,128)(2,1)} %bitcast.10, ...), custom_call_target="tpu_custom_call" | custom-call | flops 10871635968 | bytes 20971520 | tf_op jit(solution)/shard_map/pallas_call | solution.py:656
  99.9 0.8 copy.13
  100.7 0.8 copy.14
  101.5 0.6 copy.16
  102.0 2.2 %copy.15 = bf16[1,384,6144]{2,1,0:T(8,128)(2,1)} copy(bf16[1,384,6144]{2,1,0:T(8,128)(2,1)S(1)} %bitcast.7) | data formatting | bytes 9437184

commit v6 on v5

--- a/solution.py
+++ b/solution.py
@@ -560,7 +560,7 @@
     @task
     def sums_b():
         add_sums((2, 6))
-        ES[...] = EC[...].T[0:16, :]
+        ES[...] = EC[...].T[0:16, :].astype(BF)
         pltpu.make_async_copy(ES, ER.at[c], group_sem.at[E_IN]).start()
         for e in (2, 1, 3, 0):
             for r in range(2):
@@ -571,9 +571,9 @@
     @task
     def gi():
         arrived(ER, group_sem.at[E_IN], group_sem.at[E_OUT])
-        total = ER[0]
+        total = ER[0].astype(F32)
         for k in range(1, 16):
-            total = total + ER[k]
+            total = total + ER[k].astype(F32)
         QC[0:16, :] = total * (1.0 / D)
         EC[...] = jnp.zeros(EC.shape, F32)
         for b in range(8):
@@ -695,8 +695,8 @@
             v((8, 8, 128), F32),
             v((8, 2, 8, 128), F32),
             v((128, 128), F32),
-            v((16, 128), F32),
-            v((16, 16, 128), F32),
+            v((16, 128), BF),
+            v((16, 16, 128), BF),
             v((128, 128), F32),
             v((128, 128), F32),
             pltpu.SemaphoreType.DMA((128,)),

time: 104 us -> 104 us (level)
  no operation moved by 1% of the time
where the time goes in v6:
time: 104 us
  Pallas kernels  98.8 us (95%)
  local copies, waits for them, and re-layouts  4.38 us (4%)
    pallas_call x1, Pallas kernels, local(): pl.pallas_call(kernel, out_shape=tuple((v(out.shape, out.dtype) for out i...  98.8 us
    unnamed x4, local copies, waits for them, and re-layouts  4.38 us

profile of v6, /device:TPU:1, one launch (start us, length us, event | category | flops | bytes accessed | tf_op | source)
XLA Modules:
  0.0 103.8 jit_solution(11604089138774069993)
XLA Ops:
  0.6 98.8 %shard_map.84 = (bf16[48,6144]{1,0:T(8,128)(2,1)S(1)}, bf16[48,6144]{1,0:T(8,128)(2,1)S(1)}, bf16[384,6144]{1,0:T(8,128)(2,1)S(1)}, f32[1,384]{1,0:T(1,128)S(1)}) custom-call(bf16[48,6144]{1,0:T(8,128)(2,1)} %bitcast.11, bf16[48,6144]{1,0:T(8,128)(2,1)} %bitcast.12, bf16[48,6144]{1,0:T(8,128)(2,1)} %bitcast.13, bf16[384,6144]{1,0:T(8,128)(2,1)} %bitcast.10, ...), custom_call_target="tpu_custom_call" | custom-call | flops 10871635968 | bytes 20971520 | tf_op jit(solution)/shard_map/pallas_call | solution.py:656
  99.4 0.8 copy.13
  100.2 0.8 copy.14
  101.1 0.6 copy.16
  101.6 2.2 %copy.15 = bf16[1,384,6144]{2,1,0:T(8,128)(2,1)} copy(bf16[1,384,6144]{2,1,0:T(8,128)(2,1)S(1)} %bitcast.7) | data formatting | bytes 9437184

commit v7 on v6

--- a/solution.py
+++ b/solution.py
@@ -230,7 +230,7 @@
             QC[rows, :] = jnp.broadcast_to(recip, (STRIP, 128))
 
         strips(ROWS, body)
-        QS[...] = QC[...].T[0:8, :]
+        QS[...] = QC[...].T[0:1, :]
 
     def s_task(e, r):
         def run():
@@ -691,9 +691,9 @@
             v((CHIP, CA), BF),
             v((CHIP, CB), BF),
             v((128, 128), F32),
-            v((8, 128), F32),
-            v((8, 8, 128), F32),
-            v((8, 2, 8, 128), F32),
+            v((1, 128), F32),
+            v((8, 1, 128), F32),
+            v((8, 2, 1, 128), F32),
             v((128, 128), F32),
             v((16, 128), BF),
             v((16, 16, 128), BF),

time: 104 us -> 104 us (level)
  no operation moved by 1% of the time
where the time goes in v7:
time: 104 us; the launch traced here: 103 us
  Pallas kernels  98.5 us (95%)
  local copies, waits for them, and re-layouts  4.38 us (4%)
    pallas_call x1, Pallas kernels, local(): pl.pallas_call(kernel, out_shape=tuple((v(out.shape, out.dtype) for out i...  98.5 us
    unnamed x4, local copies, waits for them, and re-layouts  4.38 us

profile of v7, /device:TPU:1, one launch (start us, length us, event | category | flops | bytes accessed | tf_op | source)
XLA Modules:
  0.0 103.5 jit_solution(3147042868524914982)
XLA Ops:
  0.6 98.5 %shard_map.84 = (bf16[48,6144]{1,0:T(8,128)(2,1)S(1)}, bf16[48,6144]{1,0:T(8,128)(2,1)S(1)}, bf16[384,6144]{1,0:T(8,128)(2,1)S(1)}, f32[1,384]{1,0:T(1,128)S(1)}) custom-call(bf16[48,6144]{1,0:T(8,128)(2,1)} %bitcast.11, bf16[48,6144]{1,0:T(8,128)(2,1)} %bitcast.12, bf16[48,6144]{1,0:T(8,128)(2,1)} %bitcast.13, bf16[384,6144]{1,0:T(8,128)(2,1)} %bitcast.10, ...), custom_call_target="tpu_custom_call" | custom-call | flops 10871635968 | bytes 20971520 | tf_op jit(solution)/shard_map/pallas_call | solution.py:656
  99.1 0.8 copy.13
  99.9 0.8 copy.14
  100.7 0.6 copy.16
  101.3 2.2 %copy.15 = bf16[1,384,6144]{2,1,0:T(8,128)(2,1)} copy(bf16[1,384,6144]{2,1,0:T(8,128)(2,1)S(1)} %bitcast.7) | data formatting | bytes 9437184
